TPU v7x, 32 devices: a whole 2x2x4 slice. The times are simulated.
32 devices in a mesh: gx: 4 (over y, core), gy: 2 (over x), gz: 4 (over z).
Axes of the slice: x: 2, y: 2, z: 4, core: 2. Of those that a mesh axis runs over, the one named last changes fastest.
Arguments:
- fields: float32 [5, 64, 64, 256], P(None, 'gz', 'gx', 'gy'), may hold values from -6 to 6
- tile_writer: int32 [4, 2, 320, 1], P('gx', 'gy', 'gz'), may hold values from 0 to 7; in each aligned block of 80 rows (0 to 79, 80 to 159, ..., all dimensions but the last counted through in order) at most 15 rows name the same one
Outputs:
- coarse_bands: float32 [5, 8, 8, 32], P(None, None, 'gx', 'gy')
- received: float32 [960, 8192], P(('gx', 'gy'), 'gz')
Inputs may be any that keep to these rules, and one draw needn't show every extreme that they name: `tile_writer`: within each device's 80 entries, no destination is named more than 15 times, a bound that some block reaches.
All inputs are finite; a program needn't handle non-finite values.
Results may differ from a plain program's by a relative error of at most 0.00014.
Values sent between devices are 32-bit elements; how exact they have to be, the bound alone decides.
A program may use at most 64 MiB of HBM per device.

v0:
```python
import jax
import jax.numpy as jnp
from jax import lax
from jax.sharding import PartitionSpec as P

TILE_ROWS = 16


PREDICT_ONE = -1.586134342059924
UPDATE_ONE = -0.052980118572961
PREDICT_TWO = 0.882911075530934
UPDATE_TWO = 0.443506852043971
LOW_SCALE = 1.0 / 1.149604398860241
HIGH_SCALE = 1.149604398860241


def with_halo(block, sides, width):
    for axis, dim in sides:
        count = lax.axis_size(axis)
        forward = [(i, i + 1) for i in range(count - 1)]
        forward.append((count - 1, 0))
        backward = [(target, source) for source, target in forward]
        low = lax.ppermute(
            lax.slice_in_dim(block, block.shape[dim] - width, None, axis=dim), axis, forward
        )
        high = lax.ppermute(lax.slice_in_dim(block, 0, width, axis=dim), axis, backward)
        block = jnp.concatenate([low, block, high], axis=dim)
    return block


def lifting(values, along):
    length = values.shape[along]
    low_band = lax.slice_in_dim(values, 0, length, 2, along)
    high_band = lax.slice_in_dim(values, 1, length, 2, along)
    high_band = high_band + PREDICT_ONE * (low_band + jnp.roll(low_band, -1, along))
    low_band = low_band + UPDATE_ONE * (jnp.roll(high_band, 1, along) + high_band)
    high_band = high_band + PREDICT_TWO * (low_band + jnp.roll(low_band, -1, along))
    low_band = low_band + UPDATE_TWO * (jnp.roll(high_band, 1, along) + high_band)
    low_band = low_band * LOW_SCALE
    high_band = high_band * HIGH_SCALE
    joined = jnp.stack([low_band, high_band], axis=along + 1)
    return joined.reshape(values.shape)


def transform_matrix(length):
    identity = jnp.eye(length + 8, dtype=jnp.float32)
    return lifting(identity, 1)[:, 4:-4]


def apply_along(values, length, dim):
    matrix = transform_matrix(length)
    if dim == 1:
        return jnp.einsum("fzxy,zk->fkxy", values, matrix, precision=lax.Precision.HIGHEST)
    if dim == 2:
        return jnp.einsum("fzxy,xk->fzky", values, matrix, precision=lax.Precision.HIGHEST)
    return jnp.einsum("fzxy,yk->fzxk", values, matrix, precision=lax.Precision.HIGHEST)


def one_level(bricks):
    depth_z = bricks.shape[1]
    depth_x = bricks.shape[2]
    depth_y = bricks.shape[3]
    padded = with_halo(bricks, (("gx", 2), ("gy", 3), ("gz", 1)), 4)
    result = apply_along(padded, depth_y, 3)
    result = apply_along(result, depth_x, 2)
    return apply_along(result, depth_z, 1)


def body(fields, tile_writer):
    results = []
    current = fields
    for depth in range(3):
        result = one_level(current)
        results.append(result)
        current = result[:, ::2, ::2, ::2]
    merged = results[2]
    for depth in (1, 0):
        merged = results[depth].at[:, ::2, ::2, ::2].set(merged)
    gathered = lax.all_gather(current, "gz", axis=1, tiled=True)
    level_four = lifting(gathered, 1)
    level_five = lifting(level_four[:, ::2], 1)
    coarse_bands = level_four.at[:, ::2].set(level_five)
    width = TILE_ROWS * merged.shape[3]
    tile_rows = merged.reshape(-1, width)
    count = tile_rows.shape[0]
    groups = lax.axis_size("gx") * lax.axis_size("gy")
    capacity = max(2, 7 * count // (5 * groups) + 1)
    writers = tile_writer.reshape(count)
    onehot = (writers[:, None] == jnp.arange(groups, dtype=jnp.int32)[None, :]).astype(jnp.int32)
    slots = jnp.sum((jnp.cumsum(onehot, axis=0) - onehot) * onehot, axis=1)
    targets = writers * capacity + slots
    outbox = jnp.zeros((groups * capacity, width), jnp.float32).at[targets].set(tile_rows)
    inbox = lax.all_to_all(outbox, ("gx", "gy"), split_axis=0, concat_axis=0, tiled=True)
    return (coarse_bands, inbox)


def solution(mesh):
    return jax.shard_map(
        body,
        mesh=mesh,
        in_specs=(P(None, "gz", "gx", "gy"), P("gx", "gy", "gz", None)),
        out_specs=(P(None, None, "gx", "gy"), P(("gx", "gy"), "gz")),
        check_vma=False,
    )
```

profile of v0, /device:TPU:0, one launch (start us, length us, event | category | flops | bytes accessed | tf_op | source)
XLA Modules:
  0.0 228.1 jit_solution(2308538581642090218)
XLA Ops:
  2.4 2.0 collective-permute-start.1
  15.1 2.3 collective-permute-start.2
  23.0 2.5 %collective-permute-done.3 = f32[5,16,24,4]{2,1,3,0:T(8,128)S(1)} collective-permute-done((f32[5,16,24,4]{2,1,3,0:T(8,128)S(1)}, f32[5,16,24,4]{2,1,3,0:T(8,128)S(1)}, u32[]{:S(2)}, u32[]{:S(2)}) %collective-permute-start.3) | collective-permute-done | bytes 30752 | tf_op jit(solution)/shard_map/ppermute | solution.py:26
  29.1 2.2 collective-permute-start.5
  31.7 12.1 %collective-permute-done.4 = f32[5,4,24,136]{3,2,1,0:T(8,128)} collective-permute-done((f32[5,4,24,136]{3,2,1,0:T(8,128)}, f32[5,4,24,136]{3,2,1,0:T(8,128)}, u32[]{:S(2)}, u32[]{:S(2)}) %collective-permute-start.4) | collective-permute-done | bytes 261152 | tf_op jit(solution)/shard_map/ppermute | solution.py:23
  43.8 8.0 %collective-permute-done.5 = f32[5,4,24,136]{3,2,1,0:T(8,128)} collective-permute-done((f32[5,4,24,136]{3,2,1,0:T(8,128)}, f32[5,4,24,136]{3,2,1,0:T(8,128)}, u32[]{:S(2)}, u32[]{:S(2)}) %collective-permute-start.5) | collective-permute-done | bytes 261152 | tf_op jit(solution)/shard_map/ppermute | solution.py:26
  51.8 4.1 %fusion = f32[5,24,24,128]{3,2,1,0:T(8,128)S(1)} fusion(f32[5,4,24,136]{3,2,1,0:T(8,128)} %collective-permute-done.5, f32[5,16,24,4]{3,2,1,0:T(8,128)S(1)} %copy.51, f32[5,16,4,128]{3,2,1,0:T(4,128)S(1)} %collective-permute-done.1, f32[5,16,16,128]{3,2,1,0:T(8,128)S(1)} %copy-done, f32[5,16,4,128]{3,2,1,0:T(4,128)S(1)} %collective-permute-done, ...), kind=kOutput, calls=%fused_computation.4 | convolution fusion | flops 603970560 | bytes 5076992 | tf_op jit(solution)/shard_map/fzxy,yk->fzxk/dot_general | solution.py:56
  57.9 5.9 %slice.463 = f32[5,8,8,64]{3,1,2,0:T(8,128)S(1)} slice(f32[5,16,16,128]{3,1,2,0:T(8,128)S(1)} %bitcast.135), slice={[0:5:1], [0:16:2], [0:16:2], [0:128:2]} | slice | bytes 163840 | tf_op jit(solution)/shard_map/slice | solution.py:75
  65.7 3.0 %collective-permute-done.6 = f32[5,8,4,64]{3,1,2,0:T(8,128)S(1)} collective-permute-done((f32[5,8,4,64]{3,1,2,0:T(8,128)S(1)}, f32[5,8,4,64]{3,1,2,0:T(8,128)S(1)}, u32[]{:S(2)}, u32[]{:S(2)}) %collective-permute-start.6) | collective-permute-done | bytes 40992 | tf_op jit(solution)/shard_map/ppermute | solution.py:23
  71.0 8.4 %collective-permute-done.8 = f32[5,8,16,4]{3,1,2,0:T(8,128)S(1)} collective-permute-done((f32[5,8,16,4]{3,1,2,0:T(8,128)S(1)}, f32[5,8,16,4]{3,1,2,0:T(8,128)S(1)}, u32[]{:S(2)}, u32[]{:S(2)}) %collective-permute-start.8) | collective-permute-done | bytes 10272 | tf_op jit(solution)/shard_map/ppermute | solution.py:23
  79.5 6.2 %collective-permute-done.9 = f32[5,8,16,4]{3,1,2,0:T(8,128)S(1)} collective-permute-done((f32[5,8,16,4]{3,1,2,0:T(8,128)S(1)}, f32[5,8,16,4]{3,1,2,0:T(8,128)S(1)}, u32[]{:S(2)}, u32[]{:S(2)}) %collective-permute-start.9) | collective-permute-done | bytes 10272 | tf_op jit(solution)/shard_map/ppermute | solution.py:26
  87.4 2.5 %collective-permute-start.11 = (f32[5,4,16,72]{3,1,2,0:T(4,128)S(1)}, f32[5,4,16,72]{3,1,2,0:T(4,128)S(1)}, u32[]{:S(2)}, u32[]{:S(2)}) collective-permute-start(f32[5,4,16,72]{3,1,2,0:T(4,128)S(1)} %get-tuple-element.25), channel_id=1, source_target_pairs={{1,0},{2,1},{3,2},{0,3},{5,4},{6,5},{7,6},{4,7},{9,8},{10,9},{11,1... | collective-permute-start | bytes 276488 | tf_op jit(solution)/shard_map/ppermute | solution.py:26
  89.9 5.1 %collective-permute-done.10 = f32[5,4,16,72]{3,1,2,0:T(4,128)S(1)} collective-permute-done((f32[5,4,16,72]{3,1,2,0:T(4,128)S(1)}, f32[5,4,16,72]{3,1,2,0:T(4,128)S(1)}, u32[]{:S(2)}, u32[]{:S(2)}) %collective-permute-start.10) | collective-permute-done | bytes 92192 | tf_op jit(solution)/shard_map/ppermute | solution.py:23
  98.0 2.3 %slice.481 = f32[5,4,4,32]{3,1,2,0:T(4,128)S(1)} slice(f32[5,8,8,64]{3,1,2,0:T(8,128)S(1)} %convolution_bitcast_fusion.2), slice={[0:5:1], [0:8:2], [0:8:2], [0:64:2]} | slice | bytes 20480 | tf_op jit(solution)/shard_map/slice | solution.py:75
  106.1 3.8 %collective-permute-done.14 = f32[5,4,12,4]{3,1,2,0:T(4,128)S(1)} collective-permute-done((f32[5,4,12,4]{3,1,2,0:T(4,128)S(1)}, f32[5,4,12,4]{3,1,2,0:T(4,128)S(1)}, u32[]{:S(2)}, u32[]{:S(2)}) %collective-permute-start.14) | collective-permute-done | bytes 3872 | tf_op jit(solution)/shard_map/ppermute | solution.py:23
  109.9 2.6 %collective-permute-done.15 = f32[5,4,12,4]{3,1,2,0:T(4,128)S(1)} collective-permute-done((f32[5,4,12,4]{3,1,2,0:T(4,128)S(1)}, f32[5,4,12,4]{3,1,2,0:T(4,128)S(1)}, u32[]{:S(2)}, u32[]{:S(2)}) %collective-permute-start.15) | collective-permute-done | bytes 3872 | tf_op jit(solution)/shard_map/ppermute | solution.py:26
  113.1 3.5 %collective-permute-start.17 = (f32[5,4,12,40]{3,1,2,0:T(4,128)S(1)}, f32[5,4,12,40]{3,1,2,0:T(4,128)S(1)}, u32[]{:S(2)}, u32[]{:S(2)}) collective-permute-start(f32[5,4,12,40]{3,1,2,0:T(4,128)S(1)} %pad_maximum_fusion.12), channel_id=1, source_target_pairs={{1,0},{2,1},{3,2},{0,3},{5,4},{6,5},{7,6},{4,7},{9,8},{10,9},{11,1... | collective-permute-start | bytes 115208 | tf_op jit(solution)/shard_map/ppermute | solution.py:26
  116.8 8.6 %copy.78 = f32[16,16,128,5]{3,2,1,0:T(8,128)} copy(f32[16,16,128,5]{2,0,1,3:T(8,128)S(1)} %bitcast.136) | data formatting | bytes 1310720
  128.7 13.1 %all_gather.3 = f32[5,8,2,16]{3,2,0,1:T(2,128)S(1)} all-gather(f32[5,2,2,16]{3,2,0,1:T(2,128)S(1)} %copy.61), channel_id=1, replica_groups=mesh['gx'=4,'gy'=2,'gz'=4] {'gz'}, dimensions={1}, use_global_device_ids=true | all-gather | bytes 6400 | tf_op jit(solution)/shard_map/all_gather | solution.py:79
  142.8 31.2 %scatter_fusion.1 = f32[5,8,8,64]{0,3,2,1:T(8,128)S(1)} fusion(f32[5,8,8,64]{0,3,2,1:T(8,128)S(1)} %copy.68, s32[512]{0:T(512)S(1)} %reshape.94, f32[512,5]{1,0:T(8,128)S(1)} %bitcast.143), kind=kCustom, calls=%fused_computation.1 | custom fusion | bytes 36864 | tf_op jit(solution)/shard_map/scatter | solution.py:78
  174.0 22.1 %scatter_fusion.2 = f32[32768,5]{1,0:T(8,128)} fusion(f32[32768,5]{1,0:T(8,128)} %bitcast.133, s32[4096]{0:T(1024)S(1)} %reshape.108, f32[4096,5]{1,0:T(8,128)S(1)} %bitcast.137), kind=kCustom, calls=%fused_computation.3 | custom fusion | bytes 262144
  196.1 10.0 %copy.71 = f32[5,16,16,128]{3,2,1,0:T(8,128)S(1)} copy(f32[5,16,16,128]{0,3,2,1:T(8,128)} %bitcast.134) | data formatting | bytes 1310720 | tf_op jit(solution)/shard_map/scatter | solution.py:78
  208.6 3.6 %all-to-all-start = ((f32[8,15,2048]{2,1,0:T(8,128)}), f32[8,15,2048]{2,1,0:T(8,128)S(1)}, u32[]{:S(2)}, u32[]{:S(2)}) async-start(f32[8,15,2048]{2,1,0:T(8,128)} %all_to_all.8), calls=%async_computation | async-start | bytes 2097152 | tf_op jit(solution)/shard_map/all_to_all | solution.py:93
  213.2 13.8 %all-to-all-done = f32[8,15,2048]{2,1,0:T(8,128)S(1)} async-done(((f32[8,15,2048]{2,1,0:T(8,128)}), f32[8,15,2048]{2,1,0:T(8,128)S(1)}, u32[]{:S(2)}, u32[]{:S(2)}) %all-to-all-start) | async-done | bytes 983072 | tf_op jit(solution)/shard_map/all_to_all | solution.py:93
  (225 shorter events, 47.4 us)
Async XLA Ops:
  1.9 12.2 %collective-permute-start = (f32[5,16,4,128]{3,2,1,0:T(4,128)S(1)}, f32[5,16,4,128]{3,2,1,0:T(4,128)S(1)}, u32[]{:S(2)}, u32[]{:S(2)}) collective-permute-start(f32[5,16,4,128]{3,2,1,0:T(4,128)S(1)} %get-tuple-element.22), channel_id=1, source_target_pairs={{0,8},{8,16},{16,24},{24,0},{1,9},{9,17},{17,25},{25,1},{2,10},{10... | collective-permute-start | bytes 491528 | tf_op jit(solution)/shard_map/ppermute | solution.py:23
  2.4 11.7 %collective-permute-start.1 = (f32[5,16,4,128]{3,2,1,0:T(4,128)S(1)}, f32[5,16,4,128]{3,2,1,0:T(4,128)S(1)}, u32[]{:S(2)}, u32[]{:S(2)}) collective-permute-start(f32[5,16,4,128]{3,2,1,0:T(4,128)S(1)} %get-tuple-element.23), channel_id=1, source_target_pairs={{8,0},{16,8},{24,16},{0,24},{9,1},{17,9},{25,17},{1,25},{10,2},{18... | collective-permute-start | bytes 491528 | tf_op jit(solution)/shard_map/ppermute | solution.py:26
  15.1 7.3 %collective-permute-start.2 = (f32[5,16,24,4]{2,1,3,0:T(8,128)S(1)}, f32[5,16,24,4]{2,1,3,0:T(8,128)S(1)}, u32[]{:S(2)}, u32[]{:S(2)}) collective-permute-start(f32[5,16,24,4]{2,1,3,0:T(8,128)S(1)} %copy.48), channel_id=1, source_target_pairs={{0,4},{4,0},{1,5},{5,1},{2,6},{6,2},{3,7},{7,3},{8,12},{12,8},{9,1... | collective-permute-start | bytes 92168 | tf_op jit(solution)/shard_map/ppermute | solution.py:23
  18.0 7.4 %collective-permute-start.3 = (f32[5,16,24,4]{2,1,3,0:T(8,128)S(1)}, f32[5,16,24,4]{2,1,3,0:T(8,128)S(1)}, u32[]{:S(2)}, u32[]{:S(2)}) collective-permute-start(f32[5,16,24,4]{2,1,3,0:T(8,128)S(1)} %copy.49), channel_id=1, source_target_pairs={{4,0},{0,4},{5,1},{1,5},{6,2},{2,6},{7,3},{3,7},{12,8},{8,12},{13,... | collective-permute-start | bytes 92168 | tf_op jit(solution)/shard_map/ppermute | solution.py:26
  27.5 16.3 %collective-permute-start.4 = (f32[5,4,24,136]{3,2,1,0:T(8,128)}, f32[5,4,24,136]{3,2,1,0:T(8,128)}, u32[]{:S(2)}, u32[]{:S(2)}) collective-permute-start(f32[5,4,24,136]{3,2,1,0:T(8,128)} %get-tuple-element.18), channel_id=1, source_target_pairs={{0,1},{1,2},{2,3},{3,0},{4,5},{5,6},{6,7},{7,4},{8,9},{9,10},{10,1... | collective-permute-start | bytes 783368 | tf_op jit(solution)/shard_map/ppermute | solution.py:23
  29.1 22.7 %collective-permute-start.5 = (f32[5,4,24,136]{3,2,1,0:T(8,128)}, f32[5,4,24,136]{3,2,1,0:T(8,128)}, u32[]{:S(2)}, u32[]{:S(2)}) collective-permute-start(f32[5,4,24,136]{3,2,1,0:T(8,128)} %get-tuple-element.19), channel_id=1, source_target_pairs={{1,0},{2,1},{3,2},{0,3},{5,4},{6,5},{7,6},{4,7},{9,8},{10,9},{11,1... | collective-permute-start | bytes 783368 | tf_op jit(solution)/shard_map/ppermute | solution.py:26
  56.0 15.0 %copy-start.6 = (f32[16,8,1]{0,1,2:T(8,128)S(1)}, f32[16,8,1]{0,1,2:T(8,128)}, u32[]{:S(2)}) copy-start(f32[16,8,1]{0,1,2:T(8,128)} %get-tuple-element.10) | copy-start | bytes 1540
  56.0 15.0 %copy-start.7 = (f32[16,8,1]{0,1,2:T(8,128)S(1)}, f32[16,8,1]{0,1,2:T(8,128)}, u32[]{:S(2)}) copy-start(f32[16,8,1]{0,1,2:T(8,128)} %fusion.119) | copy-start | bytes 1540
  63.9 4.8 %collective-permute-start.6 = (f32[5,8,4,64]{3,1,2,0:T(8,128)S(1)}, f32[5,8,4,64]{3,1,2,0:T(8,128)S(1)}, u32[]{:S(2)}, u32[]{:S(2)}) collective-permute-start(f32[5,8,4,64]{3,1,2,0:T(8,128)S(1)} %get-tuple-element.28), channel_id=1, source_target_pairs={{0,8},{8,16},{16,24},{24,0},{1,9},{9,17},{17,25},{25,1},{2,10},{10... | collective-permute-start | bytes 122888 | tf_op jit(solution)/shard_map/ppermute | solution.py:23
  63.9 4.7 %collective-permute-start.7 = (f32[5,8,4,64]{3,1,2,0:T(8,128)S(1)}, f32[5,8,4,64]{3,1,2,0:T(8,128)S(1)}, u32[]{:S(2)}, u32[]{:S(2)}) collective-permute-start(f32[5,8,4,64]{3,1,2,0:T(8,128)S(1)} %get-tuple-element.29), channel_id=1, source_target_pairs={{8,0},{16,8},{24,16},{0,24},{9,1},{17,9},{25,17},{1,25},{10,2},{18... | collective-permute-start | bytes 122888 | tf_op jit(solution)/shard_map/ppermute | solution.py:26
  68.8 10.6 %collective-permute-start.8 = (f32[5,8,16,4]{3,1,2,0:T(8,128)S(1)}, f32[5,8,16,4]{3,1,2,0:T(8,128)S(1)}, u32[]{:S(2)}, u32[]{:S(2)}) collective-permute-start(f32[5,8,16,4]{3,1,2,0:T(8,128)S(1)} %get-tuple-element.26), channel_id=1, source_target_pairs={{0,4},{4,0},{1,5},{5,1},{2,6},{6,2},{3,7},{7,3},{8,12},{12,8},{9,1... | collective-permute-start | bytes 30728 | tf_op jit(solution)/shard_map/ppermute | solution.py:23
  70.2 15.5 %collective-permute-start.9 = (f32[5,8,16,4]{3,1,2,0:T(8,128)S(1)}, f32[5,8,16,4]{3,1,2,0:T(8,128)S(1)}, u32[]{:S(2)}, u32[]{:S(2)}) collective-permute-start(f32[5,8,16,4]{3,1,2,0:T(8,128)S(1)} %get-tuple-element.27), channel_id=1, source_target_pairs={{4,0},{0,4},{5,1},{1,5},{6,2},{2,6},{7,3},{3,7},{12,8},{8,12},{13,... | collective-permute-start | bytes 30728 | tf_op jit(solution)/shard_map/ppermute | solution.py:26
  85.9 20.1 %copy-start.4 = (f32[12,6,1]{0,1,2:T(8,128)S(1)}, f32[12,6,1]{0,1,2:T(8,128)}, u32[]{:S(2)}) copy-start(f32[12,6,1]{0,1,2:T(8,128)} %get-tuple-element.6) | copy-start | bytes 868
  86.0 20.1 %copy-start.5 = (f32[12,6,1]{0,1,2:T(8,128)S(1)}, f32[12,6,1]{0,1,2:T(8,128)}, u32[]{:S(2)}) copy-start(f32[12,6,1]{0,1,2:T(8,128)} %fusion.109) | copy-start | bytes 868
  86.0 9.0 %collective-permute-start.10 = (f32[5,4,16,72]{3,1,2,0:T(4,128)S(1)}, f32[5,4,16,72]{3,1,2,0:T(4,128)S(1)}, u32[]{:S(2)}, u32[]{:S(2)}) collective-permute-start(f32[5,4,16,72]{3,1,2,0:T(4,128)S(1)} %get-tuple-element.24), channel_id=1, source_target_pairs={{0,1},{1,2},{2,3},{3,0},{4,5},{5,6},{6,7},{7,4},{8,9},{9,10},{10,1... | collective-permute-start | bytes 276488 | tf_op jit(solution)/shard_map/ppermute | solution.py:23
  87.4 8.6 %collective-permute-start.11 = (f32[5,4,16,72]{3,1,2,0:T(4,128)S(1)}, f32[5,4,16,72]{3,1,2,0:T(4,128)S(1)}, u32[]{:S(2)}, u32[]{:S(2)}) collective-permute-start(f32[5,4,16,72]{3,1,2,0:T(4,128)S(1)} %get-tuple-element.25), channel_id=1, source_target_pairs={{1,0},{2,1},{3,2},{0,3},{5,4},{6,5},{7,6},{4,7},{9,8},{10,9},{11,1... | collective-permute-start | bytes 276488 | tf_op jit(solution)/shard_map/ppermute | solution.py:26
  89.9 26.7 %copy-start.2 = (s32[4,4,32,1]{2,1,0,3:T(4,128)S(1)}, s32[4,4,32,1]{2,1,0,3:T(4,128)}, u32[]{:S(2)}) copy-start(s32[4,4,32,1]{2,1,0,3:T(4,128)} %or_select_fusion) | copy-start | bytes 6148
  100.3 3.5 %collective-permute-start.12 = (f32[5,4,4,32]{3,1,2,0:T(4,128)S(1)}, f32[5,4,4,32]{3,1,2,0:T(4,128)S(1)}, u32[]{:S(2)}, u32[]{:S(2)}) collective-permute-start(f32[5,4,4,32]{3,1,2,0:T(4,128)S(1)} %slice.481), channel_id=1, source_target_pairs={{0,8},{8,16},{16,24},{24,0},{1,9},{9,17},{17,25},{25,1},{2,10},{10... | collective-permute-start | bytes 30728 | tf_op jit(solution)/shard_map/ppermute | solution.py:23
  100.4 3.4 %collective-permute-start.13 = (f32[5,4,4,32]{3,1,2,0:T(4,128)S(1)}, f32[5,4,4,32]{3,1,2,0:T(4,128)S(1)}, u32[]{:S(2)}, u32[]{:S(2)}) collective-permute-start(f32[5,4,4,32]{3,1,2,0:T(4,128)S(1)} %slice.481), channel_id=1, source_target_pairs={{8,0},{16,8},{24,16},{0,24},{9,1},{17,9},{25,17},{1,25},{10,2},{18... | collective-permute-start | bytes 30728 | tf_op jit(solution)/shard_map/ppermute | solution.py:26
  104.0 5.9 %collective-permute-start.14 = (f32[5,4,12,4]{3,1,2,0:T(4,128)S(1)}, f32[5,4,12,4]{3,1,2,0:T(4,128)S(1)}, u32[]{:S(2)}, u32[]{:S(2)}) collective-permute-start(f32[5,4,12,4]{3,1,2,0:T(4,128)S(1)} %get-tuple-element.30), channel_id=1, source_target_pairs={{0,4},{4,0},{1,5},{5,1},{2,6},{6,2},{3,7},{7,3},{8,12},{12,8},{9,1... | collective-permute-start | bytes 11528 | tf_op jit(solution)/shard_map/ppermute | solution.py:23
  105.1 7.4 %collective-permute-start.15 = (f32[5,4,12,4]{3,1,2,0:T(4,128)S(1)}, f32[5,4,12,4]{3,1,2,0:T(4,128)S(1)}, u32[]{:S(2)}, u32[]{:S(2)}) collective-permute-start(f32[5,4,12,4]{3,1,2,0:T(4,128)S(1)} %get-tuple-element.31), channel_id=1, source_target_pairs={{4,0},{0,4},{5,1},{1,5},{6,2},{2,6},{7,3},{3,7},{12,8},{8,12},{13,... | collective-permute-start | bytes 11528 | tf_op jit(solution)/shard_map/ppermute | solution.py:26
  112.7 13.4 %collective-permute-start.16 = (f32[5,4,12,40]{3,1,2,0:T(4,128)S(1)}, f32[5,4,12,40]{3,1,2,0:T(4,128)S(1)}, u32[]{:S(2)}, u32[]{:S(2)}) collective-permute-start(f32[5,4,12,40]{3,1,2,0:T(4,128)S(1)} %pad_maximum_fusion.12), channel_id=1, source_target_pairs={{0,1},{1,2},{2,3},{3,0},{4,5},{5,6},{6,7},{7,4},{8,9},{9,10},{10,1... | collective-permute-start | bytes 115208 | tf_op jit(solution)/shard_map/ppermute | solution.py:23
  113.1 13.0 %collective-permute-start.17 = (f32[5,4,12,40]{3,1,2,0:T(4,128)S(1)}, f32[5,4,12,40]{3,1,2,0:T(4,128)S(1)}, u32[]{:S(2)}, u32[]{:S(2)}) collective-permute-start(f32[5,4,12,40]{3,1,2,0:T(4,128)S(1)} %pad_maximum_fusion.12), channel_id=1, source_target_pairs={{1,0},{2,1},{3,2},{0,3},{5,4},{6,5},{7,6},{4,7},{9,8},{10,9},{11,1... | collective-permute-start | bytes 115208 | tf_op jit(solution)/shard_map/ppermute | solution.py:26
  208.6 18.4 %all-to-all-start = ((f32[8,15,2048]{2,1,0:T(8,128)}), f32[8,15,2048]{2,1,0:T(8,128)S(1)}, u32[]{:S(2)}, u32[]{:S(2)}) async-start(f32[8,15,2048]{2,1,0:T(8,128)} %all_to_all.8), calls=%async_computation | async-start | bytes 2097152 | tf_op jit(solution)/shard_map/all_to_all | solution.py:93
  (8 other events, 90.7 us)
where the time goes:
time: 229 us; the launch traced here: 228 us
  local copies, waits for them, and re-layouts  96.4 us (42%)
  waiting for transfers between devices  69.8 us (30%)
  starting transfers between devices  27.8 us (12%)
  blocking collectives  13.1 us (6%)
  other arithmetic  10.6 us (5%)
  matrix products  8.72 us (4%)
    scatter x2, local copies, waits for them, and re-layouts, body(): merged = results[depth].at[:, ::2, ::2, ::2].set(merged)  41.3 us
    ppermute x9, waiting for transfers between devices, with_halo(): lax.ppermute(lax.slice_in_dim(block, block.shape[dim] - width, None, axis...  35.6 us
    unnamed x29, local copies, waits for them, and re-layouts  30.8 us
    ppermute x9, waiting for transfers between devices, with_halo(): lax.ppermute(lax.slice_in_dim(block, 0, width, axis=dim), axis, backward)  20.4 us
    ppermute x9, starting transfers between devices, with_halo(): lax.ppermute(lax.slice_in_dim(block, 0, width, axis=dim), axis, backward)  15.5 us
    all_to_all x1, waiting for transfers between devices, body(): lax.all_to_all(outbox, ('gx', 'gy'), split_axis=0, concat_axis=0, tiled=T...  13.8 us
    all_gather x1, blocking collectives, body(): gathered = lax.all_gather(current, 'gz', axis=1, tiled=True)  13.1 us
    slice x4, local copies, waits for them, and re-layouts, body(): current = result[:, ::2, ::2, ::2]  9.31 us
  transfers between devices with their start and end apart: 19, of which 13 were waited for; matrix products, arithmetic and copies ran while one was open for 11% of the time, Pallas kernels for 0%

commit v1 on v0

v1 whole, which is shorter than its diff:
```python
import functools

import jax
import jax.numpy as jnp
from jax import lax
from jax.experimental import pallas as pl
from jax.experimental.pallas import tpu as pltpu
from jax.sharding import PartitionSpec as P

P1 = -1.586134342059924
U1 = -0.052980118572961
P2 = 0.882911075530934
U2 = 0.443506852043971
LOW = 1.0 / 1.149604398860241
HIGH = 1.149604398860241
LEVELS = 3


def coefficients(axis, step, row, lane):
    pos, other = (row, lane) if axis == 0 else (lane, row)
    active = other % step == 0
    high = active & (pos % (2 * step) == step)
    low = active & (pos % (2 * step) == 0)
    one = lambda where, value: jnp.where(where, jnp.float32(value), jnp.float32(0.0))
    scale = jnp.where(high, jnp.float32(HIGH), jnp.where(low, jnp.float32(LOW), jnp.float32(1.0)))
    return one(high, P1), one(low, U1), one(high, P2), one(low, U2), scale


def lift_in_place(v, axis, step, a, b, c, e, coefs, first, last):
    size = v.shape[axis]
    down = lambda u: pltpu.roll(u, step, axis)
    up = lambda u: pltpu.roll(u, size - step, axis)
    cp1, cu1, cp2, cu2, scale = coefs
    v1 = v + cp1 * (down(v) + jnp.where(last, c, up(v)))
    dm = a + P1 * v
    v2 = v1 + cu1 * (jnp.where(first, dm, down(v1)) + up(v1))
    sm = b + U1 * dm
    sp = e + U1 * v2
    v3 = v2 + cp2 * (down(v2) + jnp.where(last, sp, up(v2)))
    dm2 = dm + P2 * (sm + v2)
    v4 = v3 + cu2 * (jnp.where(first, dm2, down(v3)) + up(v3))
    return v4 * scale


def edge_sums(get, n):
    a = get(n - 1) + P1 * get(n - 2)
    before = get(n - 3) + P1 * (get(n - 4) + get(n - 2))
    b = get(n - 2) + U1 * before
    c = get(0)
    after = get(1) + P1 * (c + get(2))
    e = c + U1 * after
    return (a, b), (c, e)


def lift_layers(v, a, b, c, e):
    s, d = list(v[0::2]), list(v[1::2])
    n = len(s)
    s_end = [c]
    d = [d[i] + P1 * (s[i] + (s + s_end)[i + 1]) for i in range(n)]
    dm = a + P1 * s[0]
    sm = b + U1 * dm
    s_top = e + U1 * d[-1]
    s = [s[i] + U1 * (([dm] + d)[i] + d[i]) for i in range(n)]
    d = [d[i] + P2 * (s[i] + (s + [s_top])[i + 1]) for i in range(n)]
    dm = dm + P2 * (sm + s[0])
    s = [s[i] + U2 * (([dm] + d)[i] + d[i]) for i in range(n)]
    out = []
    for i in range(n):
        out += [s[i] * LOW, d[i] * HIGH]
    return out


def lift_whole(v):
    s, d = list(v[0::2]), list(v[1::2])
    n = len(s)
    d = [d[i] + P1 * (s[i] + s[(i + 1) % n]) for i in range(n)]
    s = [s[i] + U1 * (d[i - 1] + d[i]) for i in range(n)]
    d = [d[i] + P2 * (s[i] + s[(i + 1) % n]) for i in range(n)]
    s = [s[i] + U2 * (d[i - 1] + d[i]) for i in range(n)]
    out = []
    for i in range(n):
        out += [s[i] * LOW, d[i] * HIGH]
    return out


def kernel(sizes, source_ref, fields_ref, coarse_ref, inbox_ref, work, outbox, *scratch):
    n_gx, n_gy, n_gz, n_f, bz, capacity = sizes
    xs, xr, ys, yr, zs, zr = [scratch[LEVELS * i:LEVELS * (i + 1)] for i in range(6)]
    gs, gr, send, recv, g_send, g_recv, a_send, a_recv, own_sem = scratch[6 * LEVELS:]
    groups = n_gx * n_gy
    ix, iy, iz = lax.axis_index("gx"), lax.axis_index("gy"), lax.axis_index("gz")
    me = ix * n_gy + iy
    place = {"gx": (ix, n_gx), "gy": (iy, n_gy), "gz": (iz, n_gz)}

    barrier = pltpu.get_barrier_semaphore()

    def greet_plane(k, carry):
        w = lax.rem(me + k, groups)
        pl.semaphore_signal(barrier, inc=1, device_id={"gx": w // n_gy, "gy": lax.rem(w, n_gy)},
                            device_id_type=pl.DeviceIdType.MESH)
        return carry

    lax.fori_loop(1, groups, greet_plane, 0)
    for k in range(1, n_gz):
        pl.semaphore_signal(barrier, inc=1, device_id={"gz": lax.rem(iz + k, n_gz)},
                            device_id_type=pl.DeviceIdType.MESH)
    pl.semaphore_wait(barrier, groups - 1 + n_gz - 1)

    def exchange(level, kind, f, way):
        axis = ("gx", "gy", "gz")[kind]
        index, count = place[axis]
        target = lax.rem(index + (1 if way == 0 else count - 1), count)
        out, into = ((xs, xr), (ys, yr), (zs, zr))[kind]
        src = out[level].at[f] if kind == 1 else out[level].at[way, f]
        row = level * 3 + kind
        return pltpu.make_async_remote_copy(
            src_ref=src, dst_ref=into[level].at[way, f],
            send_sem=send.at[row, way, f], recv_sem=recv.at[row, way, f],
            device_id={axis: target}, device_id_type=pl.DeviceIdType.MESH)

    row = lax.broadcasted_iota(jnp.int32, (16, 128), 0)
    lane = lax.broadcasted_iota(jnp.int32, (16, 128), 1)

    def send_x(level, f, tiles):
        step = 1 << level
        for i, tile in enumerate(tiles):
            get = lambda k: tile[k * step:k * step + 1, :]
            for way, pair in enumerate(edge_sums(get, 16 // step)):
                for j in range(2):
                    xs[level][way, f, i, j:j + 1, :] = pair[j]
        for way in range(2):
            exchange(level, 0, f, way).start()

    def send_y(level, f, tiles):
        step = 1 << level
        pack = jnp.zeros((16, 128), jnp.float32)
        for i, v in enumerate(tiles):
            r1, r2 = pltpu.roll(v, step, 1), pltpu.roll(v, 128 - step, 1)
            t = U1 * (v + P1 * (r1 + r2))
            c = jnp.where(lane == 0, v, jnp.where(lane == step, r1 + t, jnp.where(
                lane == 128 - 3 * step, r2 + t, v + P1 * r1)))
            at = i * 8 * step
            moved = pltpu.roll(c, (at + 3 * step) % 128, 1)
            pack = jnp.where((lane >= at) & (lane < at + 8 * step), moved, pack)
        ys[level][f] = pack
        for way in range(2):
            exchange(level, 1, f, way).start()

    def send_z(level, f, tiles):
        for way, pair in enumerate(edge_sums(lambda k: tiles[k], len(tiles))):
            for j in range(2):
                zs[level][way, f, j] = pair[j]
        for way in range(2):
            exchange(level, 2, f, way).start()

    def planes(f, step, ref):
        return [ref[f * bz + z] if ref is work else ref[f, z] for z in range(0, bz, step)]

    def put(f, step, tiles):
        for i, tile in enumerate(tiles):
            work[f * bz + i * step] = tile

    def loop(body):
        def run(f, carry):
            body(f)
            return carry
        lax.fori_loop(0, n_f, run, 0)

    loop(lambda f: send_x(0, f, planes(f, 1, fields_ref)))
    for level in range(LEVELS):
        step = 1 << level

        def x_stage(f, level=level, step=step):
            coefs = coefficients(0, step, row, lane)
            tiles = planes(f, step, fields_ref if level == 0 else work)
            for way in range(2):
                exchange(level, 0, f, way).wait_recv()
            done = []
            for i, v in enumerate(tiles):
                a, b = [xr[level][0, f, i, j:j + 1, :] for j in range(2)]
                c, e = [xr[level][1, f, i, j:j + 1, :] for j in range(2)]
                done.append(lift_in_place(v, 0, step, a, b, c, e, coefs, row == 0, row == 16 - step))
            put(f, step, done)
            send_y(level, f, done)

        loop(x_stage)

        def y_stage(f, level=level, step=step):
            coefs = coefficients(1, step, row, lane)
            for way in range(2):
                exchange(level, 1, f, way).wait_recv()
            below, above = yr[level][0, f], yr[level][1, f]
            done = []
            for i, v in enumerate(planes(f, step, work)):
                at = i * 8 * step
                turn = lambda u, k: pltpu.roll(u, k % 128, 1) if k % 128 else u
                a, b = turn(below, -at - 2 * step), turn(below, -at)
                c, e = turn(above, -at - 4 * step), turn(above, -at - 5 * step)
                done.append(lift_in_place(v, 1, step, a, b, c, e, coefs, lane == 0, lane == 128 - step))
            put(f, step, done)
            send_z(level, f, done)

        loop(y_stage)

        def z_stage(f, level=level, step=step):
            old = planes(f, step, work)
            for way in range(2):
                exchange(level, 2, f, way).wait_recv()
            a, b = zr[level][0, f, 0], zr[level][0, f, 1]
            c, e = zr[level][1, f, 0], zr[level][1, f, 1]
            new = lift_layers(old, a, b, c, e)
            if step > 1:
                live = (row % step == 0) & (lane % step == 0)
                new = [jnp.where(live, n, o) for n, o in zip(new, old)]
            put(f, step, new)
            if level + 1 < LEVELS:
                send_x(level + 1, f, new[::2])
            else:
                for i, tile in enumerate(new[::2]):
                    for j in range(2):
                        gs[f, i, j:j + 1, :] = tile[8 * j:8 * j + 1, :]

        loop(z_stage)

    def gather(k):
        return pltpu.make_async_remote_copy(
            src_ref=gs, dst_ref=gr.at[iz], send_sem=g_send.at[k], recv_sem=g_recv.at[k],
            device_id={"gz": lax.rem(iz + k, n_gz)}, device_id_type=pl.DeviceIdType.MESH)

    for k in range(1, n_gz):
        gather(k).start()
    gr[iz] = gs[...]

    work[n_f * bz] = jnp.zeros((16, 128), jnp.float32)

    def route(k):
        w = lax.rem(me + k, groups)
        return pltpu.make_async_remote_copy(
            src_ref=outbox.at[w], dst_ref=inbox_ref.at[me], send_sem=a_send.at[k], recv_sem=a_recv.at[k],
            device_id={"gx": w // n_gy, "gy": lax.rem(w, n_gy)}, device_id_type=pl.DeviceIdType.MESH)

    def pack(w):
        for r in range(capacity):
            outbox[w, r] = work[source_ref[w * capacity + r]]

    def pack_and_send(k, carry):
        pack(lax.rem(me + k, groups))
        route(k).start()
        return carry

    lax.fori_loop(1, groups, pack_and_send, 0)
    pack(me)
    own = pltpu.make_async_copy(outbox.at[me], inbox_ref.at[me], own_sem)
    own.start()

    for k in range(1, n_gz):
        gather(k).wait_recv()
    for f in range(n_f):
        column = [gr[g, f, i] for g in range(n_gz) for i in range(2)]
        four = lift_whole(column)
        four[::2] = lift_whole(four[::2])
        for z, tile in enumerate(four):
            coarse_ref[f, z] = tile

    def finish(k, carry):
        route(k).wait()
        return carry

    lax.fori_loop(1, groups, finish, 0)
    own.wait()
    for k in range(1, n_gz):
        gather(k).wait_send()

    def sent(f):
        for level in range(LEVELS):
            for kind in range(3):
                for way in range(2):
                    exchange(level, kind, f, way).wait_send()

    loop(sent)


def source_table(writers, groups, capacity):
    count = writers.shape[0]
    place = jnp.arange(count, dtype=jnp.int32)
    same = (writers[:, None] == writers[None, :]) & (place[None, :] < place[:, None])
    targets = writers * capacity + jnp.sum(same.astype(jnp.int32), axis=1)
    slots = jnp.arange(groups * capacity, dtype=jnp.int32)
    hit = (targets[None, :] == slots[:, None]).astype(jnp.int32)
    return count - jnp.sum(hit * (count - place)[None, :], axis=1)


def body(fields, tile_writer):
    n_gx, n_gy, n_gz = lax.axis_size("gx"), lax.axis_size("gy"), lax.axis_size("gz")
    n_f, bz, bx, by = fields.shape
    count = n_f * bz
    groups = n_gx * n_gy
    capacity = max(2, 7 * count // (5 * groups) + 1)
    source = source_table(tile_writer.reshape(count), groups, capacity)
    f32 = jnp.float32
    steps = [1 << level for level in range(LEVELS)]
    scratch = [pltpu.VMEM((count + 1, bx, by), f32), pltpu.VMEM((groups, capacity, bx, by), f32)]
    scratch += [pltpu.VMEM((2, n_f, bz // s, 2, by), f32) for s in steps] * 2
    scratch += [pltpu.VMEM((n_f, bx, by), f32) for s in steps]
    scratch += [pltpu.VMEM((2, n_f, bx, by), f32) for s in steps]
    scratch += [pltpu.VMEM((2, n_f, 2, bx, by), f32) for s in steps] * 2
    scratch += [pltpu.VMEM((n_f, 2, 2, by), f32), pltpu.VMEM((n_gz, n_f, 2, 2, by), f32)]
    scratch += [pltpu.SemaphoreType.DMA((3 * LEVELS, 2, n_f))] * 2
    scratch += [pltpu.SemaphoreType.DMA((n_gz,))] * 2 + [pltpu.SemaphoreType.DMA((groups,))] * 2
    scratch += [pltpu.SemaphoreType.DMA]
    coarse, inbox = pl.pallas_call(
        functools.partial(kernel, (n_gx, n_gy, n_gz, n_f, bz, capacity)),
        out_shape=(jax.ShapeDtypeStruct((n_f, 2 * n_gz, 2, by), f32),
                   jax.ShapeDtypeStruct((groups, capacity, bx, by), f32)),
        in_specs=[pl.BlockSpec(memory_space=pltpu.SMEM), pl.BlockSpec(memory_space=pltpu.VMEM)],
        out_specs=(pl.BlockSpec(memory_space=pltpu.VMEM), pl.BlockSpec(memory_space=pl.ANY)),
        scratch_shapes=scratch,
        compiler_params=pltpu.CompilerParams(collective_id=0, has_side_effects=True,
                                             vmem_limit_bytes=32 * 1024 * 1024),
    )(source, fields)
    return coarse[..., ::8], inbox.reshape(groups * capacity, bx * by)


def solution(mesh):
    return jax.shard_map(
        body,
        mesh=mesh,
        in_specs=(P(None, "gz", "gx", "gy"), P("gx", "gy", "gz", None)),
        out_specs=(P(None, None, "gx", "gy"), P(("gx", "gy"), "gz")),
        check_vma=False,
    )
```

time: 229 us -> 60.9 us (0.27)
  local copies, waits for them, and re-layouts: 96.4 us -> 5.16 us
  waiting for transfers between devices: 69.8 us -> 0 us
  Pallas kernels: 0 us -> 54.6 us
  starting transfers between devices: 27.8 us -> 0 us
  blocking collectives: 13.1 us -> 0 us
  other arithmetic: 10.6 us -> 0.29 us
  matrix products: 8.72 us -> 0 us
    ppermute x18 -> x0, waiting for transfers between devices: 56 us -> none  [the longest x9 35.6 us: with_halo(): lax.ppermute(lax.slice_in_dim(block, block.shape[dim] - width, None, axis...]
    pallas_call x0 -> x1, Pallas kernels: none -> 54.6 us  [body(): pl.pallas_call(functools.partial(kernel, (n_gx, n_gy, n_gz, n_f, bz, capa...]
    scatter x4 -> x0, local copies, waits for them, and re-layouts: 43.4 us -> none  [the longest x2 41.3 us: body(): merged = results[depth].at[:, ::2, ::2, ::2].set(merged)]
    unnamed x29 -> x5, local copies, waits for them, and re-layouts: 30.8 us -> 2.98 us
    ppermute x18 -> x0, starting transfers between devices: 24.2 us -> none  [the longest x9 15.5 us: with_halo(): lax.ppermute(lax.slice_in_dim(block, 0, width, axis=dim), axis, backward)]
    all_to_all x1 -> x0, waiting for transfers between devices: 13.8 us -> none  [body(): lax.all_to_all(outbox, ('gx', 'gy'), split_axis=0, concat_axis=0, tiled=T...]
    slice x74 -> x1, local copies, waits for them, and re-layouts: 16 us -> 2.17 us  [body(): return (coarse[..., ::8], inbox.reshape(groups * capacity, bx * by))]
    all_gather x1 -> x0, blocking collectives: 13.1 us -> none  [body(): gathered = lax.all_gather(current, 'gz', axis=1, tiled=True)]
  transfers between devices with their start and end apart: 19 -> 0, of which waited for: 13 -> 0; matrix products, arithmetic and copies ran while one was open for 11% -> 0% of each run, Pallas kernels for 0% -> 0%
where the time goes in v1:
time: 60.9 us; the launch traced here: 60.7 us
  Pallas kernels  54.6 us (90%)
  local copies, waits for them, and re-layouts  5.16 us (8%)
  between operations  0.67 us (1%)
    pallas_call x1, Pallas kernels, body(): pl.pallas_call(functools.partial(kernel, (n_gx, n_gy, n_gz, n_f, bz, capa...  54.6 us
    unnamed x5, local copies, waits for them, and re-layouts  2.98 us
    slice x1, local copies, waits for them, and re-layouts, body(): return (coarse[..., ::8], inbox.reshape(groups * capacity, bx * by))  2.17 us

profile of v1, /device:TPU:0, one launch (start us, length us, event | category | flops | bytes accessed | tf_op | source)
XLA Modules:
  0.0 60.7 jit_solution(18228482981902603820)
XLA Ops:
  0.6 0.0 copy-start.1
  0.6 0.6 %copy-done.1 = s32[1,1,80,1]{2,3,1,0:T(1,128)S(1)} copy-done((s32[1,1,80,1]{2,3,1,0:T(1,128)S(1)}, s32[1,1,80,1]{2,3,1,0:T(1,128)}, u32[]{:S(2)}) %copy-start.1) | copy-done | bytes 344
  1.3 0.2 convert_reduce_fusion
  1.5 0.1 select_reduce_fusion
  1.6 0.0 copy-start
  1.6 1.1 %copy-done = f32[5,16,16,128]{3,2,1,0:T(8,128)S(1)} copy-done((f32[5,16,16,128]{3,2,1,0:T(8,128)S(1)}, f32[5,16,16,128]{3,2,1,0:T(8,128)}, u32[]{:S(2)}) %copy-start) | copy-done | bytes 655384
  2.7 54.6 %shard_map.41 = (f32[5,8,2,128]{3,2,1,0:T(2,128)S(1)}, f32[8,15,16,128]{3,2,1,0:T(8,128)S(1)}) custom-call(s32[120]{0:T(128)S(1)} %broadcast_subtract_fusion.source_ref, f32[5,16,16,128]{3,2,1,0:T(8,128)S(1)} %copy-done), custom_call_target="tpu_custom_call" | custom-call | tf_op jit(solution)/shard_map/pallas_call | solution.py:311
  57.3 2.2 %slice.3 = f32[5,8,2,16]{3,2,1,0:T(2,128)} slice(f32[5,8,2,128]{3,2,1,0:T(2,128)S(1)} %get-tuple-element.4), slice={[0:5:1], [0:8:1], [0:2:1], [0:128:8]} | slice | bytes 10240 | tf_op jit(solution)/shard_map/slice | solution.py:321
  59.4 1.3 %copy.6 = f32[15,8,16,128]{3,1,2,0:T(8,128)} copy(f32[15,8,16,128]{3,2,1,0:T(8,128)S(1)} %bitcast.7) | data formatting | bytes 1966080
  (2 shorter events, 0.0 us)
Async XLA Ops:
  0.6 0.7 %copy-start.1 = (s32[1,1,80,1]{2,3,1,0:T(1,128)S(1)}, s32[1,1,80,1]{2,3,1,0:T(1,128)}, u32[]{:S(2)}) copy-start(s32[1,1,80,1]{2,3,1,0:T(1,128)} %param.3) | copy-start | bytes 964
  1.6 1.1 %copy-start = (f32[5,16,16,128]{3,2,1,0:T(8,128)S(1)}, f32[5,16,16,128]{3,2,1,0:T(8,128)}, u32[]{:S(2)}) copy-start(f32[5,16,16,128]{3,2,1,0:T(8,128)} %fields_ref.1) | copy-start | bytes 1966084

commit v2 on v1

v2 whole, which is shorter than its diff:
```python
import functools

import jax
import jax.numpy as jnp
from jax import lax
from jax.experimental import pallas as pl
from jax.experimental.pallas import tpu as pltpu
from jax.sharding import PartitionSpec as P

P1 = -1.586134342059924
U1 = -0.052980118572961
P2 = 0.882911075530934
U2 = 0.443506852043971
LOW = 1.0 / 1.149604398860241
HIGH = 1.149604398860241
LEVELS = 3


def coefficients(axis, step, row, lane):
    pos, other = (row, lane) if axis == 0 else (lane, row)
    active = other % step == 0
    high = active & (pos % (2 * step) == step)
    low = active & (pos % (2 * step) == 0)
    one = lambda where, value: jnp.where(where, jnp.float32(value), jnp.float32(0.0))
    scale = jnp.where(high, jnp.float32(HIGH), jnp.where(low, jnp.float32(LOW), jnp.float32(1.0)))
    return one(high, P1), one(low, U1), one(high, P2), one(low, U2), scale


def lift_in_place(v, axis, step, a, b, c, e, coefs, first, last):
    size = v.shape[axis]
    down = lambda u: pltpu.roll(u, step, axis)
    up = lambda u: pltpu.roll(u, size - step, axis)
    cp1, cu1, cp2, cu2, scale = coefs
    v1 = v + cp1 * (down(v) + jnp.where(last, c, up(v)))
    dm = a + P1 * v
    v2 = v1 + cu1 * (jnp.where(first, dm, down(v1)) + up(v1))
    sm = b + U1 * dm
    sp = e + U1 * v2
    v3 = v2 + cp2 * (down(v2) + jnp.where(last, sp, up(v2)))
    dm2 = dm + P2 * (sm + v2)
    v4 = v3 + cu2 * (jnp.where(first, dm2, down(v3)) + up(v3))
    return v4 * scale


def edge_sums(get, n):
    a = get(n - 1) + P1 * get(n - 2)
    before = get(n - 3) + P1 * (get(n - 4) + get(n - 2))
    b = get(n - 2) + U1 * before
    c = get(0)
    after = get(1) + P1 * (c + get(2))
    e = c + U1 * after
    return (a, b), (c, e)


def lift_layers(v, a, b, c, e):
    s, d = list(v[0::2]), list(v[1::2])
    n = len(s)
    s_end = [c]
    d = [d[i] + P1 * (s[i] + (s + s_end)[i + 1]) for i in range(n)]
    dm = a + P1 * s[0]
    sm = b + U1 * dm
    s_top = e + U1 * d[-1]
    s = [s[i] + U1 * (([dm] + d)[i] + d[i]) for i in range(n)]
    d = [d[i] + P2 * (s[i] + (s + [s_top])[i + 1]) for i in range(n)]
    dm = dm + P2 * (sm + s[0])
    s = [s[i] + U2 * (([dm] + d)[i] + d[i]) for i in range(n)]
    out = []
    for i in range(n):
        out += [s[i] * LOW, d[i] * HIGH]
    return out


def lift_whole(v):
    s, d = list(v[0::2]), list(v[1::2])
    n = len(s)
    d = [d[i] + P1 * (s[i] + s[(i + 1) % n]) for i in range(n)]
    s = [s[i] + U1 * (d[i - 1] + d[i]) for i in range(n)]
    d = [d[i] + P2 * (s[i] + s[(i + 1) % n]) for i in range(n)]
    s = [s[i] + U2 * (d[i - 1] + d[i]) for i in range(n)]
    out = []
    for i in range(n):
        out += [s[i] * LOW, d[i] * HIGH]
    return out


def kernel(sizes, source_ref, fields_ref, coarse_ref, received_ref, work, outbox, inbox, *scratch):
    n_gx, n_gy, n_gz, n_f, bz, capacity = sizes
    xs, xr, ys, yr, zs, zr, cs, cr = [scratch[LEVELS * i:LEVELS * (i + 1)] for i in range(8)]
    low_rows, gs, gr, send, recv, c_send, c_recv, g_send, g_recv, a_send, a_recv, own_sem = scratch[8 * LEVELS:]
    groups = n_gx * n_gy
    ix, iy, iz = lax.axis_index("gx"), lax.axis_index("gy"), lax.axis_index("gz")
    me = ix * n_gy + iy
    place = {"gx": (ix, n_gx), "gy": (iy, n_gy), "gz": (iz, n_gz)}
    MESH = pl.DeviceIdType.MESH

    def beside(axis, way):
        index, count = place[axis]
        return lax.rem(index + (1 if way == 0 else count - 1), count)

    barrier = pltpu.get_barrier_semaphore()

    def greet_plane(k, carry):
        w = lax.rem(me + k, groups)
        pl.semaphore_signal(barrier, inc=1, device_id={"gx": w // n_gy, "gy": lax.rem(w, n_gy)},
                            device_id_type=MESH)
        return carry

    lax.fori_loop(1, groups, greet_plane, 0)
    for k in range(1, n_gz):
        pl.semaphore_signal(barrier, inc=1, device_id={"gz": lax.rem(iz + k, n_gz)}, device_id_type=MESH)
    for yway in range(2):
        for zway in range(2):
            pl.semaphore_signal(barrier, inc=1, device_id={"gy": beside("gy", yway), "gz": beside("gz", zway)},
                                device_id_type=MESH)
    pl.semaphore_wait(barrier, groups - 1 + n_gz - 1 + 4)

    def exchange(level, kind, f, way):
        axis = ("gx", "gy", "gz")[kind]
        out, into = ((xs, xr), (ys, yr), (zs, zr))[kind]
        src = out[level].at[f] if kind == 1 else out[level].at[way, f]
        row = level * 3 + kind
        return pltpu.make_async_remote_copy(
            src_ref=src, dst_ref=into[level].at[way, f],
            send_sem=send.at[row, way, f], recv_sem=recv.at[row, way, f],
            device_id={axis: beside(axis, way)}, device_id_type=MESH)

    def corner(level, yway, zway):
        return pltpu.make_async_remote_copy(
            src_ref=cs[level].at[zway], dst_ref=cr[level].at[yway, zway],
            send_sem=c_send.at[level, yway, zway], recv_sem=c_recv.at[level, yway, zway],
            device_id={"gy": beside("gy", yway), "gz": beside("gz", zway)}, device_id_type=MESH)

    row = lax.broadcasted_iota(jnp.int32, (16, 128), 0)
    lane = lax.broadcasted_iota(jnp.int32, (16, 128), 1)

    def send_x(level, f, tiles):
        step = 1 << level
        for i, tile in enumerate(tiles):
            get = lambda k: tile[k * step:k * step + 1, :]
            for way, pair in enumerate(edge_sums(get, 16 // step)):
                for j in range(2):
                    xs[level][way, f, i, j:j + 1, :] = pair[j]
        for way in range(2):
            exchange(level, 0, f, way).start()

    def spot(i, step):
        return i // step * (8 * step) + i % step

    def packed(step, pairs, pack):
        for i, v in pairs:
            r1, r2 = pltpu.roll(v, step, 1), pltpu.roll(v, 128 - step, 1)
            t = U1 * (v + P1 * (r1 + r2))
            c = jnp.where(lane == 0, v, jnp.where(lane == step, r1 + t, jnp.where(
                lane == 128 - 3 * step, r2 + t, v + P1 * r1)))
            start = i // step * (8 * step)
            here = (lane >= start) & (lane < start + 8 * step) & (lane % step == i % step)
            pack = jnp.where(here, pltpu.roll(c, (spot(i, step) + 3 * step) % 128, 1), pack)
        return pack

    def y_lift(step, i, v, below, above):
        at = spot(i, step)
        def turn(u, k):
            k = (k + 256) % 128
            return u if isinstance(k, int) and k == 0 else pltpu.roll(u, k, 1)
        a, b = turn(below, -at - 2 * step), turn(below, -at)
        c, e = turn(above, -at - 4 * step), turn(above, -at - 5 * step)
        coefs = coefficients(1, step, row, lane)
        return lift_in_place(v, 1, step, a, b, c, e, coefs, lane == 0, lane == 128 - step)

    def planes(f, step, ref):
        return [ref[f * bz + z] if ref is work else ref[f, z] for z in range(0, bz, step)]

    def put(f, step, tiles):
        for i, tile in enumerate(tiles):
            work[f * bz + i * step] = tile

    def loop(body):
        def run(f, carry):
            body(f)
            return carry
        lax.fori_loop(0, n_f, run, 0)

    def route(part, k):
        w = lax.rem(me + k, groups)
        return pltpu.make_async_remote_copy(
            src_ref=outbox.at[part, w], dst_ref=inbox.at[part, pl.ds(me * (8 * capacity), 8 * capacity)],
            send_sem=a_send.at[part, k], recv_sem=a_recv.at[part, k],
            device_id={"gx": w // n_gy, "gy": lax.rem(w, n_gy)}, device_id_type=MESH)

    def own(part):
        return pltpu.make_async_copy(
            outbox.at[part, me], inbox.at[part, pl.ds(me * (8 * capacity), 8 * capacity)], own_sem.at[part])

    def fill(part, w):
        for r in range(capacity):
            outbox[part, w, 8 * r:8 * r + 8] = work[source_ref[w * capacity + r], pl.ds(part, 8, 2), :]

    def ship(part, first, last):
        def run(k, carry):
            fill(part, lax.rem(me + k, groups))
            route(part, k).start()
            return carry
        lax.fori_loop(first, last, run, 0)

    cuts = [1 + (groups - 1) * i // 4 for i in range(5)]
    work[n_f * bz] = jnp.zeros((16, 128), jnp.float32)
    loop(lambda f: send_x(0, f, planes(f, 1, fields_ref)))
    for level in range(LEVELS):
        step = 1 << level
        if level > 0:
            ship(1, cuts[2 * level - 2], cuts[2 * level - 1])
        for zway in range(2):
            cs[level][zway] = jnp.zeros((16, 128), jnp.float32)

        def x_stage(f, level=level, step=step):
            coefs = coefficients(0, step, row, lane)
            tiles = planes(f, step, fields_ref if level == 0 else work)
            for way in range(2):
                exchange(level, 0, f, way).wait_recv()
            done = []
            for i, v in enumerate(tiles):
                a, b = [xr[level][0, f, i, j:j + 1, :] for j in range(2)]
                c, e = [xr[level][1, f, i, j:j + 1, :] for j in range(2)]
                done.append(lift_in_place(v, 0, step, a, b, c, e, coefs, row == 0, row == 16 - step))
            put(f, step, done)
            sums = edge_sums(lambda k: done[k], len(done))
            for way in range(2):
                for j in range(2):
                    zs[level][way, f, j] = sums[way][j]
                exchange(level, 2, f, way).start()
            ys[level][f] = packed(step, list(enumerate(done)), jnp.zeros((16, 128), jnp.float32))
            for way in range(2):
                exchange(level, 1, f, way).start()
            for way in range(2):
                cs[level][way] = packed(step, [(2 * f + j, sums[way][j]) for j in range(2)], cs[level][way])

        loop(x_stage)
        for yway in range(2):
            for zway in range(2):
                corner(level, yway, zway).start()
        if level > 0:
            ship(1, cuts[2 * level - 1], cuts[2 * level])

        def y_stage(f, level=level, step=step):
            for way in range(2):
                exchange(level, 1, f, way).wait_recv()
            below, above = yr[level][0, f], yr[level][1, f]
            put(f, step, [y_lift(step, i, v, below, above) for i, v in enumerate(planes(f, step, work))])

        loop(y_stage)
        for yway in range(2):
            for zway in range(2):
                corner(level, yway, zway).wait_recv()

        def z_stage(f, level=level, step=step):
            old = planes(f, step, work)
            for way in range(2):
                exchange(level, 2, f, way).wait_recv()
            edge = [[y_lift(step, 2 * f + j, zr[level][way, f, j], cr[level][0, way], cr[level][1, way])
                     for j in range(2)] for way in range(2)]
            new = lift_layers(old, *edge[0], *edge[1])
            if step > 1:
                live = (row % step == 0) & (lane % step == 0)
                new = [jnp.where(live, n, o) for n, o in zip(new, old)]
            put(f, step, new)
            if level + 1 < LEVELS:
                send_x(level + 1, f, new[::2])

        loop(z_stage)

    def gather(k):
        return pltpu.make_async_remote_copy(
            src_ref=gs, dst_ref=gr.at[iz], send_sem=g_send.at[k], recv_sem=g_recv.at[k],
            device_id={"gz": lax.rem(iz + k, n_gz)}, device_id_type=MESH)

    for i in range(2):
        for f in range(n_f):
            for j in range(2):
                low_rows[16 * i + 2 * f + j:16 * i + 2 * f + j + 1, :] = work[f * bz + 8 * i, 8 * j:8 * j + 1, :]
        low_rows[16 * i + 2 * n_f:16 * i + 16, :] = jnp.zeros((16 - 2 * n_f, 128), jnp.float32)
    pick = jnp.where(lax.broadcasted_iota(jnp.int32, (128, 128), 0) ==
                     8 * lax.broadcasted_iota(jnp.int32, (128, 128), 1), jnp.float32(1.0), jnp.float32(0.0))
    gs[...] = jnp.dot(low_rows[...], pick, precision=lax.Precision.HIGHEST, preferred_element_type=jnp.float32)
    for k in range(1, n_gz):
        gather(k).start()
    gr[iz] = gs[...]

    ship(0, 1, groups)
    for part in range(2):
        fill(part, me)
        own(part).start()

    for k in range(1, n_gz):
        gather(k).wait_recv()
    four = lift_whole([gr[g, 16 * i:16 * i + 16, :] for g in range(n_gz) for i in range(2)])
    four[::2] = lift_whole(four[::2])
    for z, tile in enumerate(four):
        for f in range(n_f):
            coarse_ref[f, z] = tile[2 * f:2 * f + 2, :16]

    def finish(k, carry):
        for part in range(2):
            route(part, k).wait()
        return carry

    lax.fori_loop(1, groups, finish, 0)
    for part in range(2):
        own(part).wait()

    def unpack(k, carry):
        for part in range(2):
            for x in range(8):
                at = (2 * x + part) * 128
                received_ref[pl.ds(pl.multiple_of(8 * k, 8), 8), at:at + 128] = (
                    inbox[part, pl.ds(64 * k + x, 8, 8), :])
        return carry

    lax.fori_loop(0, groups * capacity // 8, unpack, 0)
    for k in range(1, n_gz):
        gather(k).wait_send()

    def sent(f):
        for level in range(LEVELS):
            for kind in range(3):
                for way in range(2):
                    exchange(level, kind, f, way).wait_send()

    loop(sent)
    for level in range(LEVELS):
        for yway in range(2):
            for zway in range(2):
                corner(level, yway, zway).wait_send()


def source_table(writers, groups, capacity):
    count = writers.shape[0]
    place = jnp.arange(count, dtype=jnp.int32)
    same = (writers[:, None] == writers[None, :]) & (place[None, :] < place[:, None])
    targets = writers * capacity + jnp.sum(same.astype(jnp.int32), axis=1)
    slots = jnp.arange(groups * capacity, dtype=jnp.int32)
    hit = (targets[None, :] == slots[:, None]).astype(jnp.int32)
    return count - jnp.sum(hit * (count - place)[None, :], axis=1)


def body(fields, tile_writer):
    n_gx, n_gy, n_gz = lax.axis_size("gx"), lax.axis_size("gy"), lax.axis_size("gz")
    n_f, bz, bx, by = fields.shape
    count = n_f * bz
    groups = n_gx * n_gy
    capacity = max(2, 7 * count // (5 * groups) + 1)
    source = source_table(tile_writer.reshape(count), groups, capacity)
    f32 = jnp.float32
    steps = [1 << level for level in range(LEVELS)]
    scratch = [pltpu.VMEM((count + 1, bx, by), f32), pltpu.VMEM((2, groups, 8 * capacity, by), f32),
               pltpu.VMEM((2, groups * 8 * capacity, by), f32)]
    scratch += [pltpu.VMEM((2, n_f, bz // s, 2, by), f32) for s in steps] * 2
    scratch += [pltpu.VMEM((n_f, bx, by), f32) for s in steps]
    scratch += [pltpu.VMEM((2, n_f, bx, by), f32) for s in steps]
    scratch += [pltpu.VMEM((2, n_f, 2, bx, by), f32) for s in steps] * 2
    scratch += [pltpu.VMEM((2, bx, by), f32) for s in steps] + [pltpu.VMEM((2, 2, bx, by), f32) for s in steps]
    scratch += [pltpu.VMEM((32, by), f32)] * 2 + [pltpu.VMEM((n_gz, 32, by), f32)]
    scratch += [pltpu.SemaphoreType.DMA((3 * LEVELS, 2, n_f))] * 2
    scratch += [pltpu.SemaphoreType.DMA((LEVELS, 2, 2))] * 2
    scratch += [pltpu.SemaphoreType.DMA((n_gz,))] * 2 + [pltpu.SemaphoreType.DMA((2, groups))] * 2
    scratch += [pltpu.SemaphoreType.DMA((2,))]
    return pl.pallas_call(
        functools.partial(kernel, (n_gx, n_gy, n_gz, n_f, bz, capacity)),
        out_shape=(jax.ShapeDtypeStruct((n_f, 2 * n_gz, 2, by // 8), f32),
                   jax.ShapeDtypeStruct((groups * capacity, bx * by), f32)),
        in_specs=[pl.BlockSpec(memory_space=pltpu.SMEM), pl.BlockSpec(memory_space=pltpu.VMEM)],
        out_specs=(pl.BlockSpec(memory_space=pltpu.VMEM), pl.BlockSpec(memory_space=pltpu.VMEM)),
        scratch_shapes=scratch,
        compiler_params=pltpu.CompilerParams(collective_id=0, has_side_effects=True,
                                             vmem_limit_bytes=32 * 1024 * 1024),
    )(source, fields)


def solution(mesh):
    return jax.shard_map(
        body,
        mesh=mesh,
        in_specs=(P(None, "gz", "gx", "gy"), P("gx", "gy", "gz", None)),
        out_specs=(P(None, None, "gx", "gy"), P(("gx", "gy"), "gz")),
        check_vma=False,
    )
```

time: 60.9 us -> 55.2 us (0.906)
  Pallas kernels: 54.6 us -> 50.8 us
  local copies, waits for them, and re-layouts: 5.16 us -> 3.29 us
    pallas_call x1, Pallas kernels: 54.6 us -> 50.8 us  [body(): pl.pallas_call(functools.partial(kernel, (n_gx, n_gy, n_gz, n_f, bz, capa...]
    slice x1 -> x0, local copies, waits for them, and re-layouts: 2.17 us -> none  [body(): return (coarse[..., ::8], inbox.reshape(groups * capacity, bx * by))]
    unnamed x5 -> x6, local copies, waits for them, and re-layouts: 2.98 us -> 3.29 us
where the time goes in v2:
time: 55.2 us; the launch traced here: 55 us
  Pallas kernels  50.8 us (92%)
  local copies, waits for them, and re-layouts  3.29 us (6%)
  between operations  0.67 us (1%)
    pallas_call x1, Pallas kernels, body(): pl.pallas_call(functools.partial(kernel, (n_gx, n_gy, n_gz, n_f, bz, capa...  50.8 us
    unnamed x6, local copies, waits for them, and re-layouts  3.29 us

profile of v2, /device:TPU:0, one launch (start us, length us, event | category | flops | bytes accessed | tf_op | source)
XLA Modules:
  0.0 55.0 jit_solution(4213640254338659891)
XLA Ops:
  0.6 0.0 copy-start.1
  0.6 0.6 %copy-done.1 = s32[1,1,80,1]{2,3,1,0:T(1,128)S(1)} copy-done((s32[1,1,80,1]{2,3,1,0:T(1,128)S(1)}, s32[1,1,80,1]{2,3,1,0:T(1,128)}, u32[]{:S(2)}) %copy-start.1) | copy-done | bytes 344
  1.3 0.2 convert_reduce_fusion
  1.5 0.1 select_reduce_fusion
  1.6 0.0 copy-start
  1.6 1.1 %copy-done = f32[5,16,16,128]{3,2,1,0:T(8,128)S(1)} copy-done((f32[5,16,16,128]{3,2,1,0:T(8,128)S(1)}, f32[5,16,16,128]{3,2,1,0:T(8,128)}, u32[]{:S(2)}) %copy-start) | copy-done | bytes 655384
  2.7 50.8 %shard_map.41 = (f32[5,8,2,16]{3,2,1,0:T(2,128)S(1)}, f32[120,2048]{1,0:T(8,128)S(1)}) custom-call(s32[120]{0:T(128)S(1)} %broadcast_subtract_fusion.source_ref, f32[5,16,16,128]{3,2,1,0:T(8,128)S(1)} %copy-done), custom_call_target="tpu_custom_call" | custom-call | tf_op jit(solution)/shard_map/pallas_call | solution.py:366
  53.5 0.6 %copy.6 = f32[5,8,2,16]{3,2,1,0:T(2,128)} copy(f32[5,8,2,16]{3,2,1,0:T(2,128)S(1)} %get-tuple-element.6) | data formatting | bytes 10240
  54.1 0.9 %copy.7 = f32[120,2048]{1,0:T(8,128)} copy(f32[120,2048]{1,0:T(8,128)S(1)} %get-tuple-element.7) | data formatting | bytes 1966080
  (2 shorter events, 0.0 us)
Async XLA Ops:
  0.6 0.7 %copy-start.1 = (s32[1,1,80,1]{2,3,1,0:T(1,128)S(1)}, s32[1,1,80,1]{2,3,1,0:T(1,128)}, u32[]{:S(2)}) copy-start(s32[1,1,80,1]{2,3,1,0:T(1,128)} %param.3) | copy-start | bytes 964
  1.6 1.1 %copy-start = (f32[5,16,16,128]{3,2,1,0:T(8,128)S(1)}, f32[5,16,16,128]{3,2,1,0:T(8,128)}, u32[]{:S(2)}) copy-start(f32[5,16,16,128]{3,2,1,0:T(8,128)} %fields_ref.1) | copy-start | bytes 1966084

commit v3 on v2

--- a/solution.py
+++ b/solution.py
@@ -117,10 +117,15 @@
     def exchange(level, kind, f, way):
         axis = ("gx", "gy", "gz")[kind]
         out, into = ((xs, xr), (ys, yr), (zs, zr))[kind]
-        src = out[level].at[f] if kind == 1 else out[level].at[way, f]
+        src = out[level] if kind == 1 else out[level].at[way]
+        dst = into[level].at[way]
+        if level == 0:
+            src, dst = src.at[f], dst.at[f]
+        else:
+            f = 0
         row = level * 3 + kind
         return pltpu.make_async_remote_copy(
-            src_ref=src, dst_ref=into[level].at[way, f],
+            src_ref=src, dst_ref=dst,
             send_sem=send.at[row, way, f], recv_sem=recv.at[row, way, f],
             device_id={axis: beside(axis, way)}, device_id_type=MESH)
 
@@ -140,8 +145,12 @@
             for way, pair in enumerate(edge_sums(get, 16 // step)):
                 for j in range(2):
                     xs[level][way, f, i, j:j + 1, :] = pair[j]
+
+    def both(level, kind, f, act):
         for way in range(2):
-            exchange(level, 0, f, way).start()
+            act(exchange(level, kind, f, way))
+
+    start, arrive = lambda copy: copy.start(), lambda copy: copy.wait_recv()
 
     def spot(i, step):
         return i // step * (8 * step) + i % step
@@ -180,6 +189,19 @@
             return carry
         lax.fori_loop(0, n_f, run, 0)
 
+    def stage(level, body, receives, sends):
+        def run(fs, f):
+            for kind in receives:
+                both(level, kind, f, arrive)
+            for g in fs:
+                body(g)
+            for kind in sends:
+                both(level, kind, f, start)
+        if level == 0:
+            loop(lambda f: run([f], f))
+        else:
+            run(range(n_f), 0)
+
     def route(part, k):
         w = lax.rem(me + k, groups)
         return pltpu.make_async_remote_copy(
@@ -204,7 +226,7 @@
 
     cuts = [1 + (groups - 1) * i // 4 for i in range(5)]
     work[n_f * bz] = jnp.zeros((16, 128), jnp.float32)
-    loop(lambda f: send_x(0, f, planes(f, 1, fields_ref)))
+    stage(0, lambda f: send_x(0, f, planes(f, 1, fields_ref)), [], [0])
     for level in range(LEVELS):
         step = 1 << level
         if level > 0:
@@ -215,8 +237,6 @@
         def x_stage(f, level=level, step=step):
             coefs = coefficients(0, step, row, lane)
             tiles = planes(f, step, fields_ref if level == 0 else work)
-            for way in range(2):
-                exchange(level, 0, f, way).wait_recv()
             done = []
             for i, v in enumerate(tiles):
                 a, b = [xr[level][0, f, i, j:j + 1, :] for j in range(2)]
@@ -227,14 +247,11 @@
             for way in range(2):
                 for j in range(2):
                     zs[level][way, f, j] = sums[way][j]
-                exchange(level, 2, f, way).start()
             ys[level][f] = packed(step, list(enumerate(done)), jnp.zeros((16, 128), jnp.float32))
             for way in range(2):
-                exchange(level, 1, f, way).start()
-            for way in range(2):
                 cs[level][way] = packed(step, [(2 * f + j, sums[way][j]) for j in range(2)], cs[level][way])
 
-        loop(x_stage)
+        stage(level, x_stage, [0], [2, 1])
         for yway in range(2):
             for zway in range(2):
                 corner(level, yway, zway).start()
@@ -242,20 +259,16 @@
             ship(1, cuts[2 * level - 1], cuts[2 * level])
 
         def y_stage(f, level=level, step=step):
-            for way in range(2):
-                exchange(level, 1, f, way).wait_recv()
             below, above = yr[level][0, f], yr[level][1, f]
             put(f, step, [y_lift(step, i, v, below, above) for i, v in enumerate(planes(f, step, work))])
 
-        loop(y_stage)
+        stage(level, y_stage, [1], [])
         for yway in range(2):
             for zway in range(2):
                 corner(level, yway, zway).wait_recv()
 
         def z_stage(f, level=level, step=step):
             old = planes(f, step, work)
-            for way in range(2):
-                exchange(level, 2, f, way).wait_recv()
             edge = [[y_lift(step, 2 * f + j, zr[level][way, f, j], cr[level][0, way], cr[level][1, way])
                      for j in range(2)] for way in range(2)]
             new = lift_layers(old, *edge[0], *edge[1])
@@ -266,7 +279,9 @@
             if level + 1 < LEVELS:
                 send_x(level + 1, f, new[::2])
 
-        loop(z_stage)
+        stage(level, z_stage, [2], [])
+        if level + 1 < LEVELS:
+            both(level + 1, 0, 0, start)
 
     def gather(k):
         return pltpu.make_async_remote_copy(
@@ -319,13 +334,13 @@
     for k in range(1, n_gz):
         gather(k).wait_send()
 
-    def sent(f):
-        for level in range(LEVELS):
-            for kind in range(3):
-                for way in range(2):
-                    exchange(level, kind, f, way).wait_send()
-
-    loop(sent)
+    def sent(level, f):
+        for kind in range(3):
+            both(level, kind, f, lambda copy: copy.wait_send())
+
+    loop(lambda f: sent(0, f))
+    for level in range(1, LEVELS):
+        sent(level, 0)
     for level in range(LEVELS):
         for yway in range(2):
             for zway in range(2):

time: 55.2 us -> 62.6 us (1.13)
  Pallas kernels: 50.8 us -> 58.1 us
    pallas_call x1, Pallas kernels: 50.8 us -> 58.1 us  [body(): pl.pallas_call(functools.partial(kernel, (n_gx, n_gy, n_gz, n_f, bz, capa...]
where the time goes in v3:
time: 62.6 us; the launch traced here: 62.4 us
  Pallas kernels  58.1 us (93%)
  local copies, waits for them, and re-layouts  3.29 us (5%)
  between operations  0.67 us (1%)
    pallas_call x1, Pallas kernels, body(): pl.pallas_call(functools.partial(kernel, (n_gx, n_gy, n_gz, n_f, bz, capa...  58.1 us
    unnamed x6, local copies, waits for them, and re-layouts  3.29 us

profile of v3, /device:TPU:0, one launch (start us, length us, event | category | flops | bytes accessed | tf_op | source)
XLA Modules:
  0.0 62.4 jit_solution(16835392480492744542)
XLA Ops:
  0.6 0.0 copy-start.1
  0.6 0.6 %copy-done.1 = s32[1,1,80,1]{2,3,1,0:T(1,128)S(1)} copy-done((s32[1,1,80,1]{2,3,1,0:T(1,128)S(1)}, s32[1,1,80,1]{2,3,1,0:T(1,128)}, u32[]{:S(2)}) %copy-start.1) | copy-done | bytes 344
  1.3 0.2 convert_reduce_fusion
  1.5 0.1 select_reduce_fusion
  1.6 0.0 copy-start
  1.6 1.1 %copy-done = f32[5,16,16,128]{3,2,1,0:T(8,128)S(1)} copy-done((f32[5,16,16,128]{3,2,1,0:T(8,128)S(1)}, f32[5,16,16,128]{3,2,1,0:T(8,128)}, u32[]{:S(2)}) %copy-start) | copy-done | bytes 655384
  2.7 58.1 %shard_map.41 = (f32[5,8,2,16]{3,2,1,0:T(2,128)S(1)}, f32[120,2048]{1,0:T(8,128)S(1)}) custom-call(s32[120]{0:T(128)S(1)} %broadcast_subtract_fusion.source_ref, f32[5,16,16,128]{3,2,1,0:T(8,128)S(1)} %copy-done), custom_call_target="tpu_custom_call" | custom-call | tf_op jit(solution)/shard_map/pallas_call | solution.py:381
  60.8 0.6 copy.6
  61.4 0.9 %copy.7 = f32[120,2048]{1,0:T(8,128)} copy(f32[120,2048]{1,0:T(8,128)S(1)} %get-tuple-element.7) | data formatting | bytes 1966080
  (2 shorter events, 0.0 us)
Async XLA Ops:
  0.6 0.7 %copy-start.1 = (s32[1,1,80,1]{2,3,1,0:T(1,128)S(1)}, s32[1,1,80,1]{2,3,1,0:T(1,128)}, u32[]{:S(2)}) copy-start(s32[1,1,80,1]{2,3,1,0:T(1,128)} %param.3) | copy-start | bytes 964
  1.6 1.1 %copy-start = (f32[5,16,16,128]{3,2,1,0:T(8,128)S(1)}, f32[5,16,16,128]{3,2,1,0:T(8,128)}, u32[]{:S(2)}) copy-start(f32[5,16,16,128]{3,2,1,0:T(8,128)} %fields_ref.1) | copy-start | bytes 1966084

commit v4 on v2

--- a/solution.py
+++ b/solution.py
@@ -2,6 +2,7 @@
 
 import jax
 import jax.numpy as jnp
+import numpy as np
 from jax import lax
 from jax.experimental import pallas as pl
 from jax.experimental.pallas import tpu as pltpu
@@ -16,30 +17,60 @@
 LEVELS = 3
 
 
-def coefficients(axis, step, row, lane):
-    pos, other = (row, lane) if axis == 0 else (lane, row)
-    active = other % step == 0
-    high = active & (pos % (2 * step) == step)
-    low = active & (pos % (2 * step) == 0)
-    one = lambda where, value: jnp.where(where, jnp.float32(value), jnp.float32(0.0))
-    scale = jnp.where(high, jnp.float32(HIGH), jnp.where(low, jnp.float32(LOW), jnp.float32(1.0)))
-    return one(high, P1), one(low, U1), one(high, P2), one(low, U2), scale
-
-
-def lift_in_place(v, axis, step, a, b, c, e, coefs, first, last):
-    size = v.shape[axis]
-    down = lambda u: pltpu.roll(u, step, axis)
-    up = lambda u: pltpu.roll(u, size - step, axis)
-    cp1, cu1, cp2, cu2, scale = coefs
-    v1 = v + cp1 * (down(v) + jnp.where(last, c, up(v)))
-    dm = a + P1 * v
-    v2 = v1 + cu1 * (jnp.where(first, dm, down(v1)) + up(v1))
-    sm = b + U1 * dm
-    sp = e + U1 * v2
-    v3 = v2 + cp2 * (down(v2) + jnp.where(last, sp, up(v2)))
-    dm2 = dm + P2 * (sm + v2)
-    v4 = v3 + cu2 * (jnp.where(first, dm2, down(v3)) + up(v3))
-    return v4 * scale
+def lift_matrix(n, step):
+    basis = np.eye(n + 4)
+    v, (a, b, c, e) = basis[:n].copy(), basis[n:]
+    v[::step] = np.stack(lift_layers(list(v[::step]), a, b, c, e))
+    return v
+
+
+def edge_matrix(n, step):
+    below, above = edge_sums(lambda k: np.eye(n)[k * step], n // step)
+    return np.stack(below + above)
+
+
+def tiles_at_once(level):
+    return min(8, 16 >> level)
+
+
+def matrices(level):
+    step, t = 1 << level, tiles_at_once(level)
+    x_all, x_edge, y_all, y_edge = lift_matrix(16, step), edge_matrix(16, step), lift_matrix(128, step), edge_matrix(128, step)
+    mx, hx, ex = np.zeros((128, 128)), np.zeros((128, 32)), np.zeros((32, 128))
+    for i in range(t):
+        rows = slice(16 * i, 16 * i + 16)
+        mx[rows, rows] = x_all[:, :16]
+        for way in range(2):
+            edge = slice(2 * t * way + 2 * i, 2 * t * way + 2 * i + 2)
+            hx[rows, edge] = x_all[:, 16 + 2 * way:18 + 2 * way]
+            ex[edge, rows] = x_edge[2 * way:2 * way + 2]
+    mq, hy = np.zeros((128, 256)), np.zeros((128, 128))
+    mq[:, :128] = y_all[:, :128].T
+    for sum_index, offset in enumerate((2, 0, 3, 4)):
+        hy[offset * step] = y_all[:, 128 + sum_index]
+        for group in range(16):
+            mq[:, 128 + group // step * (8 * step) + group % step + offset * step] = y_edge[sum_index]
+    return mx, hx, ex, mq, hy
+
+
+def constant_tables():
+    tables = []
+    for kind in zip(*[matrices(level) for level in range(LEVELS)]):
+        whole = np.stack(kind).astype(np.float32)
+        high = whole.astype(jnp.bfloat16)
+        low = (whole - high.astype(np.float32)).astype(jnp.bfloat16)
+        tables.append(jnp.asarray(np.stack([high, low], axis=1)))
+    return tables
+
+
+def halves(v):
+    high = v.astype(jnp.bfloat16)
+    return high, (v - high.astype(jnp.float32)).astype(jnp.bfloat16)
+
+
+def product(a, b):
+    dot = lambda p, q: jnp.dot(p, q, preferred_element_type=jnp.float32)
+    return dot(a[0], b[0]) + dot(a[1], b[0]) + dot(a[0], b[1])
 
 
 def edge_sums(get, n):
@@ -83,7 +114,7 @@
     return out
 
 
-def kernel(sizes, source_ref, fields_ref, coarse_ref, received_ref, work, outbox, inbox, *scratch):
+def kernel(sizes, source_ref, fields_ref, mx_ref, hx_ref, ex_ref, mq_ref, hy_ref, coarse_ref, received_ref, work, outbox, inbox, *scratch):
     n_gx, n_gy, n_gz, n_f, bz, capacity = sizes
     xs, xr, ys, yr, zs, zr, cs, cr = [scratch[LEVELS * i:LEVELS * (i + 1)] for i in range(8)]
     low_rows, gs, gr, send, recv, c_send, c_recv, g_send, g_recv, a_send, a_recv, own_sem = scratch[8 * LEVELS:]
@@ -134,12 +165,12 @@
     lane = lax.broadcasted_iota(jnp.int32, (16, 128), 1)
 
     def send_x(level, f, tiles):
-        step = 1 << level
-        for i, tile in enumerate(tiles):
-            get = lambda k: tile[k * step:k * step + 1, :]
-            for way, pair in enumerate(edge_sums(get, 16 // step)):
-                for j in range(2):
-                    xs[level][way, f, i, j:j + 1, :] = pair[j]
+        t = tiles_at_once(level)
+        sums = tuple(ex_ref[level, half, :4 * t, :16 * t] for half in range(2))
+        for k in range(0, len(tiles), t):
+            edge = product(sums, halves(jnp.concatenate(tiles[k:k + t], axis=0)))
+            for way in range(2):
+                xs[level][way, f, 2 * k:2 * (k + t), :] = edge[2 * t * way:2 * t * (way + 1)]
         for way in range(2):
             exchange(level, 0, f, way).start()
 
@@ -148,24 +179,14 @@
 
     def packed(step, pairs, pack):
         for i, v in pairs:
-            r1, r2 = pltpu.roll(v, step, 1), pltpu.roll(v, 128 - step, 1)
-            t = U1 * (v + P1 * (r1 + r2))
-            c = jnp.where(lane == 0, v, jnp.where(lane == step, r1 + t, jnp.where(
-                lane == 128 - 3 * step, r2 + t, v + P1 * r1)))
             start = i // step * (8 * step)
             here = (lane >= start) & (lane < start + 8 * step) & (lane % step == i % step)
-            pack = jnp.where(here, pltpu.roll(c, (spot(i, step) + 3 * step) % 128, 1), pack)
+            pack = jnp.where(here, v, pack)
         return pack
 
-    def y_lift(step, i, v, below, above):
-        at = spot(i, step)
-        def turn(u, k):
-            k = (k + 256) % 128
-            return u if isinstance(k, int) and k == 0 else pltpu.roll(u, k, 1)
-        a, b = turn(below, -at - 2 * step), turn(below, -at)
-        c, e = turn(above, -at - 4 * step), turn(above, -at - 5 * step)
-        coefs = coefficients(1, step, row, lane)
-        return lift_in_place(v, 1, step, a, b, c, e, coefs, lane == 0, lane == 128 - step)
+    def edge_lanes(step, below, above, spots):
+        both = jnp.where(lane % (8 * step) // step < 3, below, above)
+        return [pltpu.roll(both, (128 - spot(i, step)) % 128, 1) for i in spots]
 
     def planes(f, step, ref):
         return [ref[f * bz + z] if ref is work else ref[f, z] for z in range(0, bz, step)]
@@ -212,25 +233,33 @@
         for zway in range(2):
             cs[level][zway] = jnp.zeros((16, 128), jnp.float32)
 
-        def x_stage(f, level=level, step=step):
-            coefs = coefficients(0, step, row, lane)
+        t = tiles_at_once(level)
+        live = (row % step == 0) & (lane % step == 0)
+
+        def x_stage(f, level=level, step=step, t=t, live=live):
             tiles = planes(f, step, fields_ref if level == 0 else work)
             for way in range(2):
                 exchange(level, 0, f, way).wait_recv()
-            done = []
-            for i, v in enumerate(tiles):
-                a, b = [xr[level][0, f, i, j:j + 1, :] for j in range(2)]
-                c, e = [xr[level][1, f, i, j:j + 1, :] for j in range(2)]
-                done.append(lift_in_place(v, 0, step, a, b, c, e, coefs, row == 0, row == 16 - step))
-            put(f, step, done)
-            sums = edge_sums(lambda k: done[k], len(done))
+            mx = tuple(mx_ref[level, half, :16 * t, :16 * t] for half in range(2))
+            hx = tuple(hx_ref[level, half, :16 * t, :4 * t] for half in range(2))
+            mq = tuple(mq_ref[level, half] for half in range(2))
+            wide = []
+            for k in range(0, len(tiles), t):
+                edge = jnp.concatenate([xr[level][way, f, 2 * k:2 * (k + t), :] for way in range(2)], axis=0)
+                lifted = product(mx, halves(jnp.concatenate(tiles[k:k + t], axis=0))) + product(hx, halves(edge))
+                lifted = product(halves(lifted), mq)
+                wide += [lifted[16 * i:16 * i + 16] for i in range(t)]
+            own_lanes, sum_lanes = [w[:, :128] for w in wide], [w[:, 128:] for w in wide]
+            put(f, step, own_lanes if step == 1 else [jnp.where(live, n, o) for n, o in zip(own_lanes, tiles)])
+            sums = edge_sums(lambda k: own_lanes[k], len(wide))
             for way in range(2):
                 for j in range(2):
                     zs[level][way, f, j] = sums[way][j]
                 exchange(level, 2, f, way).start()
-            ys[level][f] = packed(step, list(enumerate(done)), jnp.zeros((16, 128), jnp.float32))
+            ys[level][f] = packed(step, list(enumerate(sum_lanes)), jnp.zeros((16, 128), jnp.float32))
             for way in range(2):
                 exchange(level, 1, f, way).start()
+            sums = edge_sums(lambda k: sum_lanes[k], len(wide))
             for way in range(2):
                 cs[level][way] = packed(step, [(2 * f + j, sums[way][j]) for j in range(2)], cs[level][way])
 
@@ -241,26 +270,27 @@
         if level > 0:
             ship(1, cuts[2 * level - 1], cuts[2 * level])
 
-        def y_stage(f, level=level, step=step):
-            for way in range(2):
-                exchange(level, 1, f, way).wait_recv()
-            below, above = yr[level][0, f], yr[level][1, f]
-            put(f, step, [y_lift(step, i, v, below, above) for i, v in enumerate(planes(f, step, work))])
-
-        loop(y_stage)
         for yway in range(2):
             for zway in range(2):
                 corner(level, yway, zway).wait_recv()
 
-        def z_stage(f, level=level, step=step):
+        def z_stage(f, level=level, step=step, live=live):
             old = planes(f, step, work)
             for way in range(2):
+                exchange(level, 1, f, way).wait_recv()
                 exchange(level, 2, f, way).wait_recv()
-            edge = [[y_lift(step, 2 * f + j, zr[level][way, f, j], cr[level][0, way], cr[level][1, way])
-                     for j in range(2)] for way in range(2)]
-            new = lift_layers(old, *edge[0], *edge[1])
+            hy = tuple(hy_ref[level, half] for half in range(2))
+            edges = edge_lanes(step, yr[level][0, f], yr[level][1, f], range(len(old)))
+            for way in range(2):
+                edges += edge_lanes(step, cr[level][0, way], cr[level][1, way], [2 * f, 2 * f + 1])
+            extra = product(halves(jnp.concatenate(edges, axis=0)), hy)
             if step > 1:
-                live = (row % step == 0) & (lane % step == 0)
+                extra = jnp.where((lax.broadcasted_iota(jnp.int32, extra.shape, 0) % step) == 0, extra, 0.0)
+            extra = [extra[16 * i:16 * i + 16] for i in range(len(edges))]
+            edge = [zr[level][way, f, j] + extra[len(old) + 2 * way + j] for way in range(2) for j in range(2)]
+            old = [o + x for o, x in zip(old, extra)]
+            new = lift_layers(old, *edge)
+            if step > 1:
                 new = [jnp.where(live, n, o) for n, o in zip(new, old)]
             put(f, step, new)
             if level + 1 < LEVELS:
@@ -353,7 +383,7 @@
     steps = [1 << level for level in range(LEVELS)]
     scratch = [pltpu.VMEM((count + 1, bx, by), f32), pltpu.VMEM((2, groups, 8 * capacity, by), f32),
                pltpu.VMEM((2, groups * 8 * capacity, by), f32)]
-    scratch += [pltpu.VMEM((2, n_f, bz // s, 2, by), f32) for s in steps] * 2
+    scratch += [pltpu.VMEM((2, n_f, 2 * bz // s, by), f32) for s in steps] * 2
     scratch += [pltpu.VMEM((n_f, bx, by), f32) for s in steps]
     scratch += [pltpu.VMEM((2, n_f, bx, by), f32) for s in steps]
     scratch += [pltpu.VMEM((2, n_f, 2, bx, by), f32) for s in steps] * 2
@@ -367,12 +397,12 @@
         functools.partial(kernel, (n_gx, n_gy, n_gz, n_f, bz, capacity)),
         out_shape=(jax.ShapeDtypeStruct((n_f, 2 * n_gz, 2, by // 8), f32),
                    jax.ShapeDtypeStruct((groups * capacity, bx * by), f32)),
-        in_specs=[pl.BlockSpec(memory_space=pltpu.SMEM), pl.BlockSpec(memory_space=pltpu.VMEM)],
+        in_specs=[pl.BlockSpec(memory_space=pltpu.SMEM)] + [pl.BlockSpec(memory_space=pltpu.VMEM)] * 6,
         out_specs=(pl.BlockSpec(memory_space=pltpu.VMEM), pl.BlockSpec(memory_space=pltpu.VMEM)),
         scratch_shapes=scratch,
         compiler_params=pltpu.CompilerParams(collective_id=0, has_side_effects=True,
                                              vmem_limit_bytes=32 * 1024 * 1024),
-    )(source, fields)
+    )(source, fields, *constant_tables())
 
 
 def solution(mesh):

time: 55.2 us -> 58.4 us (1.058)
  local copies, waits for them, and re-layouts: 3.29 us -> 7.87 us
  Pallas kernels: 50.8 us -> 49.3 us
    unnamed x6 -> x16, local copies, waits for them, and re-layouts: 3.29 us -> 7.87 us
    pallas_call x1, Pallas kernels: 50.8 us -> 49.3 us  [body(): pl.pallas_call(functools.partial(kernel, (n_gx, n_gy, n_gz, n_f, bz, capa...]
where the time goes in v4:
time: 58.4 us; the launch traced here: 58.1 us
  Pallas kernels  49.3 us (84%)
  local copies, waits for them, and re-layouts  7.87 us (13%)
  between operations  0.67 us (1%)
    pallas_call x1, Pallas kernels, body(): pl.pallas_call(functools.partial(kernel, (n_gx, n_gy, n_gz, n_f, bz, capa...  49.3 us
    unnamed x16, local copies, waits for them, and re-layouts  7.87 us

profile of v4, /device:TPU:0, one launch (start us, length us, event | category | flops | bytes accessed | tf_op | source)
XLA Modules:
  0.0 58.1 jit_solution(9422598037320549434)
XLA Ops:
  0.6 0.0 copy-start.6
  0.6 0.6 %copy-done.6 = s32[1,1,80,1]{2,3,1,0:T(1,128)S(1)} copy-done((s32[1,1,80,1]{2,3,1,0:T(1,128)S(1)}, s32[1,1,80,1]{2,3,1,0:T(1,128)}, u32[]{:S(2)}) %copy-start.6) | copy-done | bytes 344
  1.3 0.2 convert_reduce_fusion
  1.5 0.1 select_reduce_fusion
  1.6 0.0 copy-start
  1.6 1.1 %copy-done = f32[5,16,16,128]{3,2,1,0:T(8,128)S(1)} copy-done((f32[5,16,16,128]{3,2,1,0:T(8,128)S(1)}, f32[5,16,16,128]{3,2,1,0:T(8,128)}, u32[]{:S(2)}) %copy-start) | copy-done | bytes 655384
  2.7 0.0 copy-start.1
  2.7 1.0 %copy-done.1 = bf16[3,2,128,256]{3,2,1,0:T(8,128)(2,1)S(1)} copy-done((bf16[3,2,128,256]{3,2,1,0:T(8,128)(2,1)S(1)}, bf16[3,2,128,256]{3,2,1,0:T(8,128)(2,1)}, u32[]{:S(2)}) %copy-start.1) | copy-done | bytes 393240
  3.7 0.0 copy-start.2
  3.7 0.9 %copy-done.2 = bf16[3,2,128,128]{3,2,1,0:T(8,128)(2,1)S(1)} copy-done((bf16[3,2,128,128]{3,2,1,0:T(8,128)(2,1)S(1)}, bf16[3,2,128,128]{3,2,1,0:T(8,128)(2,1)}, u32[]{:S(2)}) %copy-start.2) | copy-done | bytes 196632
  4.6 0.0 copy-start.3
  4.6 0.9 %copy-done.3 = bf16[3,2,128,32]{3,2,1,0:T(8,128)(2,1)S(1)} copy-done((bf16[3,2,128,32]{3,2,1,0:T(8,128)(2,1)S(1)}, bf16[3,2,128,32]{3,2,1,0:T(8,128)(2,1)}, u32[]{:S(2)}) %copy-start.3) | copy-done | bytes 49176
  5.5 0.0 copy-start.4
  5.5 0.9 %copy-done.4 = bf16[3,2,128,128]{3,2,1,0:T(8,128)(2,1)S(1)} copy-done((bf16[3,2,128,128]{3,2,1,0:T(8,128)(2,1)S(1)}, bf16[3,2,128,128]{3,2,1,0:T(8,128)(2,1)}, u32[]{:S(2)}) %copy-start.4) | copy-done | bytes 196632
  6.5 0.0 copy-start.5
  6.5 0.8 %copy-done.5 = bf16[3,2,32,128]{3,2,1,0:T(8,128)(2,1)S(1)} copy-done((bf16[3,2,32,128]{3,2,1,0:T(8,128)(2,1)S(1)}, bf16[3,2,32,128]{3,2,1,0:T(8,128)(2,1)}, u32[]{:S(2)}) %copy-start.5) | copy-done | bytes 49176
  7.3 49.3 %shard_map.86 = (f32[5,8,2,16]{3,2,1,0:T(2,128)S(1)}, f32[120,2048]{1,0:T(8,128)S(1)}) custom-call(s32[120]{0:T(128)S(1)} %broadcast_subtract_fusion.source_ref, f32[5,16,16,128]{3,2,1,0:T(8,128)S(1)} %copy-done, bf16[3,2,128,128]{3,2,1,0:T(8,128)(2,1)S(1)} %copy-done.4, bf16[3,2,128,32]{3,2,1,0:T(8,128)(2,1)S(1)} %copy-done.3, ...), custom_call_target="tpu_custom_call" | custom-call | tf_op jit(solution)/shard_map/pallas_call | solution.py:396
  56.5 0.6 %copy.11 = f32[5,8,2,16]{3,2,1,0:T(2,128)} copy(f32[5,8,2,16]{3,2,1,0:T(2,128)S(1)} %get-tuple-element.6) | data formatting | bytes 10240
  57.2 0.9 %copy.12 = f32[120,2048]{1,0:T(8,128)} copy(f32[120,2048]{1,0:T(8,128)S(1)} %get-tuple-element.7) | data formatting | bytes 1966080
  (2 shorter events, 0.0 us)
Async XLA Ops:
  0.6 0.7 %copy-start.6 = (s32[1,1,80,1]{2,3,1,0:T(1,128)S(1)}, s32[1,1,80,1]{2,3,1,0:T(1,128)}, u32[]{:S(2)}) copy-start(s32[1,1,80,1]{2,3,1,0:T(1,128)} %param.8) | copy-start | bytes 964
  1.6 1.1 %copy-start = (f32[5,16,16,128]{3,2,1,0:T(8,128)S(1)}, f32[5,16,16,128]{3,2,1,0:T(8,128)}, u32[]{:S(2)}) copy-start(f32[5,16,16,128]{3,2,1,0:T(8,128)} %fields_ref.1) | copy-start | bytes 1966084
  2.7 1.0 %copy-start.1 = (bf16[3,2,128,256]{3,2,1,0:T(8,128)(2,1)S(1)}, bf16[3,2,128,256]{3,2,1,0:T(8,128)(2,1)}, u32[]{:S(2)}) copy-start(bf16[3,2,128,256]{3,2,1,0:T(8,128)(2,1)} %constant.21.clone.mq_ref) | copy-start | bytes 1179652
  3.7 0.9 %copy-start.2 = (bf16[3,2,128,128]{3,2,1,0:T(8,128)(2,1)S(1)}, bf16[3,2,128,128]{3,2,1,0:T(8,128)(2,1)}, u32[]{:S(2)}) copy-start(bf16[3,2,128,128]{3,2,1,0:T(8,128)(2,1)} %constant.22.clone.hy_ref) | copy-start | bytes 589828
  4.6 0.9 %copy-start.3 = (bf16[3,2,128,32]{3,2,1,0:T(8,128)(2,1)S(1)}, bf16[3,2,128,32]{3,2,1,0:T(8,128)(2,1)}, u32[]{:S(2)}) copy-start(bf16[3,2,128,32]{3,2,1,0:T(8,128)(2,1)} %constant.19.clone.hx_ref) | copy-start | bytes 147460
  5.5 0.9 %copy-start.4 = (bf16[3,2,128,128]{3,2,1,0:T(8,128)(2,1)S(1)}, bf16[3,2,128,128]{3,2,1,0:T(8,128)(2,1)}, u32[]{:S(2)}) copy-start(bf16[3,2,128,128]{3,2,1,0:T(8,128)(2,1)} %constant.18.clone.mx_ref) | copy-start | bytes 589828
  6.5 0.8 %copy-start.5 = (bf16[3,2,32,128]{3,2,1,0:T(8,128)(2,1)S(1)}, bf16[3,2,32,128]{3,2,1,0:T(8,128)(2,1)}, u32[]{:S(2)}) copy-start(bf16[3,2,32,128]{3,2,1,0:T(8,128)(2,1)} %constant.20.clone.ex_ref) | copy-start | bytes 147460

commit v5 on v4

--- a/solution.py
+++ b/solution.py
@@ -15,6 +15,7 @@
 LOW = 1.0 / 1.149604398860241
 HIGH = 1.149604398860241
 LEVELS = 3
+PARTS = ((1, 8, 2), (2, 4, 4), (0, 4, 4))
 
 
 def lift_matrix(n, step):
@@ -114,8 +115,15 @@
     return out
 
 
-def kernel(sizes, source_ref, fields_ref, mx_ref, hx_ref, ex_ref, mq_ref, hy_ref, coarse_ref, received_ref, work, outbox, inbox, *scratch):
+def kernel(sizes, source_ref, *refs):
     n_gx, n_gy, n_gz, n_f, bz, capacity = sizes
+    given, (coarse_ref, received_ref), held, scratch = refs[:6], refs[6:8], refs[8:14], refs[14:]
+    fields_ref, mx_ref, hx_ref, ex_ref, mq_ref, hy_ref = held
+    work, turn_rows, load_sem = scratch[:3]
+    outbox, inbox, scratch = scratch[3:6], scratch[6:9], scratch[9:]
+    loads = [pltpu.make_async_copy(a, b, load_sem.at[i]) for i, (a, b) in enumerate(zip(given, held))]
+    for load in loads:
+        load.start()
     xs, xr, ys, yr, zs, zr, cs, cr = [scratch[LEVELS * i:LEVELS * (i + 1)] for i in range(8)]
     low_rows, gs, gr, send, recv, c_send, c_recv, g_send, g_recv, a_send, a_recv, own_sem = scratch[8 * LEVELS:]
     groups = n_gx * n_gy
@@ -143,6 +151,8 @@
         for zway in range(2):
             pl.semaphore_signal(barrier, inc=1, device_id={"gy": beside("gy", yway), "gz": beside("gz", zway)},
                                 device_id_type=MESH)
+    for load in loads:
+        load.wait()
     pl.semaphore_wait(barrier, groups - 1 + n_gz - 1 + 4)
 
     def exchange(level, kind, f, way):
@@ -201,20 +211,33 @@
             return carry
         lax.fori_loop(0, n_f, run, 0)
 
+    def squeeze(slot, v, step):
+        if step == 1:
+            return v
+        turn_rows[slot] = v
+        return turn_rows[slot, pl.ds(0, 16 // step, step), :]
+
+    def spread(slot, v, step):
+        if step == 1:
+            return v
+        turn_rows[slot, pl.ds(0, 16 // step, step), :] = v
+        return turn_rows[slot]
+
     def route(part, k):
         w = lax.rem(me + k, groups)
         return pltpu.make_async_remote_copy(
-            src_ref=outbox.at[part, w], dst_ref=inbox.at[part, pl.ds(me * (8 * capacity), 8 * capacity)],
+            src_ref=outbox[part].at[w], dst_ref=inbox[part].at[pl.ds(me * capacity, capacity)],
             send_sem=a_send.at[part, k], recv_sem=a_recv.at[part, k],
             device_id={"gx": w // n_gy, "gy": lax.rem(w, n_gy)}, device_id_type=MESH)
 
     def own(part):
         return pltpu.make_async_copy(
-            outbox.at[part, me], inbox.at[part, pl.ds(me * (8 * capacity), 8 * capacity)], own_sem.at[part])
+            outbox[part].at[me], inbox[part].at[pl.ds(me * capacity, capacity)], own_sem.at[part])
 
     def fill(part, w):
+        first, count, stride = PARTS[part]
         for r in range(capacity):
-            outbox[part, w, 8 * r:8 * r + 8] = work[source_ref[w * capacity + r], pl.ds(part, 8, 2), :]
+            outbox[part][w, r] = work[source_ref[w * capacity + r], pl.ds(first, count, stride), :]
 
     def ship(part, first, last):
         def run(k, carry):
@@ -223,13 +246,14 @@
             return carry
         lax.fori_loop(first, last, run, 0)
 
-    cuts = [1 + (groups - 1) * i // 4 for i in range(5)]
+    cuts = [1 + (groups - 1) * i // 2 for i in range(3)]
+    turn_rows[...] = jnp.zeros_like(turn_rows)
     work[n_f * bz] = jnp.zeros((16, 128), jnp.float32)
     loop(lambda f: send_x(0, f, planes(f, 1, fields_ref)))
     for level in range(LEVELS):
         step = 1 << level
         if level > 0:
-            ship(1, cuts[2 * level - 2], cuts[2 * level - 1])
+            ship(level - 1, cuts[0], cuts[1])
         for zway in range(2):
             cs[level][zway] = jnp.zeros((16, 128), jnp.float32)
 
@@ -253,10 +277,15 @@
             put(f, step, own_lanes if step == 1 else [jnp.where(live, n, o) for n, o in zip(own_lanes, tiles)])
             sums = edge_sums(lambda k: own_lanes[k], len(wide))
             for way in range(2):
-                for j in range(2):
-                    zs[level][way, f, j] = sums[way][j]
+                if step == 1:
+                    for j in range(2):
+                        zs[level][way, f, j] = sums[way][j]
+                else:
+                    mixed = jnp.where(lane % step == 0, sums[way][0], pltpu.roll(sums[way][1], 1, 1))
+                    zs[level][way, f] = squeeze(way, mixed, step)
                 exchange(level, 2, f, way).start()
-            ys[level][f] = packed(step, list(enumerate(sum_lanes)), jnp.zeros((16, 128), jnp.float32))
+            pack = packed(step, list(enumerate(sum_lanes)), jnp.zeros((16, 128), jnp.float32))
+            ys[level][f] = squeeze(2, pack, step)
             for way in range(2):
                 exchange(level, 1, f, way).start()
             sums = edge_sums(lambda k: sum_lanes[k], len(wide))
@@ -268,7 +297,9 @@
             for zway in range(2):
                 corner(level, yway, zway).start()
         if level > 0:
-            ship(1, cuts[2 * level - 1], cuts[2 * level])
+            ship(level - 1, cuts[1], cuts[2])
+            fill(level - 1, me)
+            own(level - 1).start()
 
         for yway in range(2):
             for zway in range(2):
@@ -280,14 +311,21 @@
                 exchange(level, 1, f, way).wait_recv()
                 exchange(level, 2, f, way).wait_recv()
             hy = tuple(hy_ref[level, half] for half in range(2))
-            edges = edge_lanes(step, yr[level][0, f], yr[level][1, f], range(len(old)))
+            edges = edge_lanes(step, spread(3, yr[level][0, f], step), spread(4, yr[level][1, f], step), range(len(old)))
             for way in range(2):
                 edges += edge_lanes(step, cr[level][0, way], cr[level][1, way], [2 * f, 2 * f + 1])
             extra = product(halves(jnp.concatenate(edges, axis=0)), hy)
             if step > 1:
                 extra = jnp.where((lax.broadcasted_iota(jnp.int32, extra.shape, 0) % step) == 0, extra, 0.0)
             extra = [extra[16 * i:16 * i + 16] for i in range(len(edges))]
-            edge = [zr[level][way, f, j] + extra[len(old) + 2 * way + j] for way in range(2) for j in range(2)]
+            far = []
+            for way in range(2):
+                if step == 1:
+                    far += [zr[level][way, f, 0], zr[level][way, f, 1]]
+                else:
+                    mixed = spread(5 + way, zr[level][way, f], step)
+                    far += [mixed, pltpu.roll(mixed, 127, 1)]
+            edge = [v + x for v, x in zip(far, extra[len(old):])]
             old = [o + x for o, x in zip(old, extra)]
             new = lift_layers(old, *edge)
             if step > 1:
@@ -315,10 +353,10 @@
         gather(k).start()
     gr[iz] = gs[...]
 
-    ship(0, 1, groups)
-    for part in range(2):
-        fill(part, me)
-        own(part).start()
+    last = len(PARTS) - 1
+    ship(last, 1, groups)
+    fill(last, me)
+    own(last).start()
 
     for k in range(1, n_gz):
         gather(k).wait_recv()
@@ -329,20 +367,19 @@
             coarse_ref[f, z] = tile[2 * f:2 * f + 2, :16]
 
     def finish(k, carry):
-        for part in range(2):
+        for part in range(len(PARTS)):
             route(part, k).wait()
         return carry
 
     lax.fori_loop(1, groups, finish, 0)
-    for part in range(2):
+    for part in range(len(PARTS)):
         own(part).wait()
 
     def unpack(k, carry):
-        for part in range(2):
-            for x in range(8):
-                at = (2 * x + part) * 128
-                received_ref[pl.ds(pl.multiple_of(8 * k, 8), 8), at:at + 128] = (
-                    inbox[part, pl.ds(64 * k + x, 8, 8), :])
+        for part, (first, count, stride) in enumerate(PARTS):
+            for x in range(count):
+                at = (first + stride * x) * 128
+                received_ref[pl.ds(pl.multiple_of(8 * k, 8), 8), at:at + 128] = inbox[part][pl.ds(8 * k, 8), x, :]
         return carry
 
     lax.fori_loop(0, groups * capacity // 8, unpack, 0)
@@ -381,28 +418,31 @@
     source = source_table(tile_writer.reshape(count), groups, capacity)
     f32 = jnp.float32
     steps = [1 << level for level in range(LEVELS)]
-    scratch = [pltpu.VMEM((count + 1, bx, by), f32), pltpu.VMEM((2, groups, 8 * capacity, by), f32),
-               pltpu.VMEM((2, groups * 8 * capacity, by), f32)]
+    tables = constant_tables()
+    scratch = [pltpu.VMEM(a.shape, a.dtype) for a in (fields, *tables)]
+    scratch += [pltpu.VMEM((count + 1, bx, by), f32), pltpu.VMEM((7, bx, by), f32), pltpu.SemaphoreType.DMA((6,))]
+    scratch += [pltpu.VMEM((groups, capacity, p[1], by), f32) for p in PARTS]
+    scratch += [pltpu.VMEM((groups * capacity, p[1], by), f32) for p in PARTS]
     scratch += [pltpu.VMEM((2, n_f, 2 * bz // s, by), f32) for s in steps] * 2
-    scratch += [pltpu.VMEM((n_f, bx, by), f32) for s in steps]
-    scratch += [pltpu.VMEM((2, n_f, bx, by), f32) for s in steps]
-    scratch += [pltpu.VMEM((2, n_f, 2, bx, by), f32) for s in steps] * 2
+    scratch += [pltpu.VMEM((n_f, bx // s, by), f32) for s in steps]
+    scratch += [pltpu.VMEM((2, n_f, bx // s, by), f32) for s in steps]
+    scratch += [pltpu.VMEM((2, n_f, 2, bx, by) if s == 1 else (2, n_f, bx // s, by), f32) for s in steps] * 2
     scratch += [pltpu.VMEM((2, bx, by), f32) for s in steps] + [pltpu.VMEM((2, 2, bx, by), f32) for s in steps]
     scratch += [pltpu.VMEM((32, by), f32)] * 2 + [pltpu.VMEM((n_gz, 32, by), f32)]
     scratch += [pltpu.SemaphoreType.DMA((3 * LEVELS, 2, n_f))] * 2
     scratch += [pltpu.SemaphoreType.DMA((LEVELS, 2, 2))] * 2
-    scratch += [pltpu.SemaphoreType.DMA((n_gz,))] * 2 + [pltpu.SemaphoreType.DMA((2, groups))] * 2
-    scratch += [pltpu.SemaphoreType.DMA((2,))]
+    scratch += [pltpu.SemaphoreType.DMA((n_gz,))] * 2 + [pltpu.SemaphoreType.DMA((len(PARTS), groups))] * 2
+    scratch += [pltpu.SemaphoreType.DMA((len(PARTS),))]
     return pl.pallas_call(
         functools.partial(kernel, (n_gx, n_gy, n_gz, n_f, bz, capacity)),
         out_shape=(jax.ShapeDtypeStruct((n_f, 2 * n_gz, 2, by // 8), f32),
                    jax.ShapeDtypeStruct((groups * capacity, bx * by), f32)),
-        in_specs=[pl.BlockSpec(memory_space=pltpu.SMEM)] + [pl.BlockSpec(memory_space=pltpu.VMEM)] * 6,
+        in_specs=[pl.BlockSpec(memory_space=pltpu.SMEM)] + [pl.BlockSpec(memory_space=pl.ANY)] * 6,
         out_specs=(pl.BlockSpec(memory_space=pltpu.VMEM), pl.BlockSpec(memory_space=pltpu.VMEM)),
         scratch_shapes=scratch,
         compiler_params=pltpu.CompilerParams(collective_id=0, has_side_effects=True,
                                              vmem_limit_bytes=32 * 1024 * 1024),
-    )(source, fields, *constant_tables())
+    )(source, fields, *tables)
 
 
 def solution(mesh):

time: 58.4 us -> 55.3 us (0.947)
  Pallas kernels: 49.3 us -> 46.2 us
    pallas_call x1, Pallas kernels: 49.3 us -> 46.2 us  [body(): pl.pallas_call(functools.partial(kernel, (n_gx, n_gy, n_gz, n_f, bz, capa...]
where the time goes in v5:
time: 55.3 us; the launch traced here: 55 us
  Pallas kernels  46.2 us (84%)
  local copies, waits for them, and re-layouts  7.87 us (14%)
  between operations  0.67 us (1%)
    pallas_call x1, Pallas kernels, body(): pl.pallas_call(functools.partial(kernel, (n_gx, n_gy, n_gz, n_f, bz, capa...  46.2 us
    unnamed x16, local copies, waits for them, and re-layouts  7.87 us

profile of v5, /device:TPU:0, one launch (start us, length us, event | category | flops | bytes accessed | tf_op | source)
XLA Modules:
  0.0 55.0 jit_solution(7721676846175644374)
XLA Ops:
  0.6 0.0 copy-start.6
  0.6 0.6 %copy-done.6 = s32[1,1,80,1]{2,3,1,0:T(1,128)S(1)} copy-done((s32[1,1,80,1]{2,3,1,0:T(1,128)S(1)}, s32[1,1,80,1]{2,3,1,0:T(1,128)}, u32[]{:S(2)}) %copy-start.6) | copy-done | bytes 344
  1.3 0.2 convert_reduce_fusion
  1.5 0.1 select_reduce_fusion
  1.6 0.0 copy-start
  1.6 1.1 %copy-done = f32[5,16,16,128]{3,2,1,0:T(8,128)S(1)} copy-done((f32[5,16,16,128]{3,2,1,0:T(8,128)S(1)}, f32[5,16,16,128]{3,2,1,0:T(8,128)}, u32[]{:S(2)}) %copy-start) | copy-done | bytes 655384
  2.7 0.0 copy-start.1
  2.7 1.0 %copy-done.1 = bf16[3,2,128,256]{3,2,1,0:T(8,128)(2,1)S(1)} copy-done((bf16[3,2,128,256]{3,2,1,0:T(8,128)(2,1)S(1)}, bf16[3,2,128,256]{3,2,1,0:T(8,128)(2,1)}, u32[]{:S(2)}) %copy-start.1) | copy-done | bytes 393240
  3.7 0.0 copy-start.2
  3.7 0.9 %copy-done.2 = bf16[3,2,128,128]{3,2,1,0:T(8,128)(2,1)S(1)} copy-done((bf16[3,2,128,128]{3,2,1,0:T(8,128)(2,1)S(1)}, bf16[3,2,128,128]{3,2,1,0:T(8,128)(2,1)}, u32[]{:S(2)}) %copy-start.2) | copy-done | bytes 196632
  4.6 0.0 copy-start.3
  4.6 0.9 %copy-done.3 = bf16[3,2,128,32]{3,2,1,0:T(8,128)(2,1)S(1)} copy-done((bf16[3,2,128,32]{3,2,1,0:T(8,128)(2,1)S(1)}, bf16[3,2,128,32]{3,2,1,0:T(8,128)(2,1)}, u32[]{:S(2)}) %copy-start.3) | copy-done | bytes 49176
  5.5 0.0 copy-start.4
  5.5 0.9 %copy-done.4 = bf16[3,2,128,128]{3,2,1,0:T(8,128)(2,1)S(1)} copy-done((bf16[3,2,128,128]{3,2,1,0:T(8,128)(2,1)S(1)}, bf16[3,2,128,128]{3,2,1,0:T(8,128)(2,1)}, u32[]{:S(2)}) %copy-start.4) | copy-done | bytes 196632
  6.5 0.0 copy-start.5
  6.5 0.8 %copy-done.5 = bf16[3,2,32,128]{3,2,1,0:T(8,128)(2,1)S(1)} copy-done((bf16[3,2,32,128]{3,2,1,0:T(8,128)(2,1)S(1)}, bf16[3,2,32,128]{3,2,1,0:T(8,128)(2,1)}, u32[]{:S(2)}) %copy-start.5) | copy-done | bytes 49176
  7.3 46.2 %shard_map.86 = (f32[5,8,2,16]{3,2,1,0:T(2,128)S(1)}, f32[120,2048]{1,0:T(8,128)S(1)}) custom-call(s32[120]{0:T(128)S(1)} %broadcast_subtract_fusion.source_ref, f32[5,16,16,128]{3,2,1,0:T(8,128)S(1)} %copy-done, bf16[3,2,128,128]{3,2,1,0:T(8,128)(2,1)S(1)} %copy-done.4, bf16[3,2,128,32]{3,2,1,0:T(8,128)(2,1)S(1)} %copy-done.3, ...), custom_call_target="tpu_custom_call" | custom-call | tf_op jit(solution)/shard_map/pallas_call | solution.py:436
  53.4 0.6 %copy.11 = f32[5,8,2,16]{3,2,1,0:T(2,128)} copy(f32[5,8,2,16]{3,2,1,0:T(2,128)S(1)} %get-tuple-element.6) | data formatting | bytes 10240
  54.1 0.9 %copy.12 = f32[120,2048]{1,0:T(8,128)} copy(f32[120,2048]{1,0:T(8,128)S(1)} %get-tuple-element.7) | data formatting | bytes 1966080
  (2 shorter events, 0.0 us)
Async XLA Ops:
  0.6 0.7 %copy-start.6 = (s32[1,1,80,1]{2,3,1,0:T(1,128)S(1)}, s32[1,1,80,1]{2,3,1,0:T(1,128)}, u32[]{:S(2)}) copy-start(s32[1,1,80,1]{2,3,1,0:T(1,128)} %param.8) | copy-start | bytes 964
  1.6 1.1 %copy-start = (f32[5,16,16,128]{3,2,1,0:T(8,128)S(1)}, f32[5,16,16,128]{3,2,1,0:T(8,128)}, u32[]{:S(2)}) copy-start(f32[5,16,16,128]{3,2,1,0:T(8,128)} %refs_0_.1) | copy-start | bytes 1966084
  2.7 1.0 %copy-start.1 = (bf16[3,2,128,256]{3,2,1,0:T(8,128)(2,1)S(1)}, bf16[3,2,128,256]{3,2,1,0:T(8,128)(2,1)}, u32[]{:S(2)}) copy-start(bf16[3,2,128,256]{3,2,1,0:T(8,128)(2,1)} %constant.21.clone.refs_4_) | copy-start | bytes 1179652
  3.7 0.9 %copy-start.2 = (bf16[3,2,128,128]{3,2,1,0:T(8,128)(2,1)S(1)}, bf16[3,2,128,128]{3,2,1,0:T(8,128)(2,1)}, u32[]{:S(2)}) copy-start(bf16[3,2,128,128]{3,2,1,0:T(8,128)(2,1)} %constant.22.clone.refs_5_) | copy-start | bytes 589828
  4.6 0.9 %copy-start.3 = (bf16[3,2,128,32]{3,2,1,0:T(8,128)(2,1)S(1)}, bf16[3,2,128,32]{3,2,1,0:T(8,128)(2,1)}, u32[]{:S(2)}) copy-start(bf16[3,2,128,32]{3,2,1,0:T(8,128)(2,1)} %constant.19.clone.refs_2_) | copy-start | bytes 147460
  5.5 0.9 %copy-start.4 = (bf16[3,2,128,128]{3,2,1,0:T(8,128)(2,1)S(1)}, bf16[3,2,128,128]{3,2,1,0:T(8,128)(2,1)}, u32[]{:S(2)}) copy-start(bf16[3,2,128,128]{3,2,1,0:T(8,128)(2,1)} %constant.18.clone.refs_1_) | copy-start | bytes 589828
  6.5 0.8 %copy-start.5 = (bf16[3,2,32,128]{3,2,1,0:T(8,128)(2,1)S(1)}, bf16[3,2,32,128]{3,2,1,0:T(8,128)(2,1)}, u32[]{:S(2)}) copy-start(bf16[3,2,32,128]{3,2,1,0:T(8,128)(2,1)} %constant.20.clone.refs_3_) | copy-start | bytes 147460

commit v6 on v5

--- a/solution.py
+++ b/solution.py
@@ -437,11 +437,11 @@
         functools.partial(kernel, (n_gx, n_gy, n_gz, n_f, bz, capacity)),
         out_shape=(jax.ShapeDtypeStruct((n_f, 2 * n_gz, 2, by // 8), f32),
                    jax.ShapeDtypeStruct((groups * capacity, bx * by), f32)),
-        in_specs=[pl.BlockSpec(memory_space=pltpu.SMEM)] + [pl.BlockSpec(memory_space=pl.ANY)] * 6,
+        in_specs=[pl.BlockSpec(memory_space=pltpu.SMEM)] + [pl.BlockSpec(memory_space=pltpu.HBM)] * 6,
         out_specs=(pl.BlockSpec(memory_space=pltpu.VMEM), pl.BlockSpec(memory_space=pltpu.VMEM)),
         scratch_shapes=scratch,
         compiler_params=pltpu.CompilerParams(collective_id=0, has_side_effects=True,
-                                             vmem_limit_bytes=32 * 1024 * 1024),
+                                             vmem_limit_bytes=60 * 1024 * 1024),
     )(source, fields, *tables)
 
 

time: 55.3 us -> 51.8 us (0.937)
  local copies, waits for them, and re-layouts: 7.87 us -> 4.28 us
    unnamed x16 -> x4, local copies, waits for them, and re-layouts: 7.87 us -> 4.28 us
where the time goes in v6:
time: 51.8 us; the launch traced here: 51.6 us
  Pallas kernels  45.8 us (88%)
  local copies, waits for them, and re-layouts  4.28 us (8%)
  other arithmetic  0.81 us (2%)
  between operations  0.66 us (1%)
    pallas_call x1, Pallas kernels, body(): pl.pallas_call(functools.partial(kernel, (n_gx, n_gy, n_gz, n_f, bz, capa...  45.8 us
    unnamed x4, local copies, waits for them, and re-layouts  4.28 us

profile of v6, /device:TPU:0, one launch (start us, length us, event | category | flops | bytes accessed | tf_op | source)
XLA Modules:
  0.0 51.6 jit_solution(794984281669672324)
XLA Ops:
  0.6 0.0 copy-start
  0.6 0.6 %copy-done = s32[1,1,80,1]{2,3,1,0:T(1,128)S(1)} copy-done((s32[1,1,80,1]{2,3,1,0:T(1,128)S(1)}, s32[1,1,80,1]{2,3,1,0:T(1,128)}, u32[]{:S(2)}) %copy-start) | copy-done | bytes 344
  1.3 0.2 convert_reduce_fusion
  1.5 0.1 select_reduce_fusion
  1.6 0.5 %broadcast_subtract_fusion.source_ref = s32[120]{0:T(128)} fusion(s32[120]{0:T(128)S(1)} %select_reduce_fusion), kind=kLoop, calls=%fused_computation.7 | loop fusion | flops 120 | bytes 960 | tf_op jit(solution)/shard_map/sub | solution.py:409
  2.1 45.8 %shard_map.86 = (f32[5,8,2,16]{3,2,1,0:T(2,128)}, f32[120,2048]{1,0:T(8,128)}) custom-call(s32[120]{0:T(128)} %broadcast_subtract_fusion.source_ref, f32[5,16,16,128]{3,2,1,0:T(8,128)} %refs_0_.1, bf16[3,2,128,128]{3,2,1,0:T(8,128)(2,1)} %constant.18.clone.refs_1_, bf16[3,2,128,32]{3,2,1,0:T(8,128)(2,1)} %constant.19.clone.refs_2_, ...), custom_call_target="tpu_custom_call" | custom-call | tf_op jit(solution)/shard_map/pallas_call | solution.py:436
  47.9 1.4 %copy.11 = f32[5,8,2,16]{3,2,1,0:T(2,128)} copy(f32[5,8,2,16]{3,2,1,0:T(2,128)} %get-tuple-element.6) | data formatting | bytes 10240
  49.3 2.2 %copy.12 = f32[120,2048]{1,0:T(8,128)} copy(f32[120,2048]{1,0:T(8,128)} %get-tuple-element.7) | data formatting | bytes 1966080
  (1 shorter events, 0.0 us)
Async XLA Ops:
  0.6 0.7 %copy-start = (s32[1,1,80,1]{2,3,1,0:T(1,128)S(1)}, s32[1,1,80,1]{2,3,1,0:T(1,128)}, u32[]{:S(2)}) copy-start(s32[1,1,80,1]{2,3,1,0:T(1,128)} %param.8) | copy-start | bytes 964

commit v7 on v6

--- a/solution.py
+++ b/solution.py
@@ -117,10 +117,10 @@
 
 def kernel(sizes, source_ref, *refs):
     n_gx, n_gy, n_gz, n_f, bz, capacity = sizes
-    given, (coarse_ref, received_ref), held, scratch = refs[:6], refs[6:8], refs[8:14], refs[14:]
+    given, coarse_ref, inbox, held, scratch = refs[:6], refs[6], refs[7:10], refs[10:16], refs[16:]
     fields_ref, mx_ref, hx_ref, ex_ref, mq_ref, hy_ref = held
     work, turn_rows, load_sem = scratch[:3]
-    outbox, inbox, scratch = scratch[3:6], scratch[6:9], scratch[9:]
+    outbox, scratch = scratch[3:6], scratch[6:]
     loads = [pltpu.make_async_copy(a, b, load_sem.at[i]) for i, (a, b) in enumerate(zip(given, held))]
     for load in loads:
         load.start()
@@ -375,14 +375,6 @@
     for part in range(len(PARTS)):
         own(part).wait()
 
-    def unpack(k, carry):
-        for part, (first, count, stride) in enumerate(PARTS):
-            for x in range(count):
-                at = (first + stride * x) * 128
-                received_ref[pl.ds(pl.multiple_of(8 * k, 8), 8), at:at + 128] = inbox[part][pl.ds(8 * k, 8), x, :]
-        return carry
-
-    lax.fori_loop(0, groups * capacity // 8, unpack, 0)
     for k in range(1, n_gz):
         gather(k).wait_send()
 
@@ -397,6 +389,21 @@
         for yway in range(2):
             for zway in range(2):
                 corner(level, yway, zway).wait_send()
+
+
+def lay_out(coarse_ref, *refs):
+    inbox, (bands_ref, received_ref) = refs[:len(PARTS)], refs[len(PARTS):]
+    bands_ref[...] = coarse_ref[...]
+
+    def unpack(k, carry):
+        rows = pl.ds(pl.multiple_of(8 * k, 8), 8)
+        for part, (first, count, stride) in enumerate(PARTS):
+            for x in range(count):
+                at = (first + stride * x) * 128
+                received_ref[rows, at:at + 128] = inbox[part][rows, x, :]
+        return carry
+
+    lax.fori_loop(0, received_ref.shape[0] // 8, unpack, 0)
 
 
 def source_table(writers, groups, capacity):
@@ -422,7 +429,6 @@
     scratch = [pltpu.VMEM(a.shape, a.dtype) for a in (fields, *tables)]
     scratch += [pltpu.VMEM((count + 1, bx, by), f32), pltpu.VMEM((7, bx, by), f32), pltpu.SemaphoreType.DMA((6,))]
     scratch += [pltpu.VMEM((groups, capacity, p[1], by), f32) for p in PARTS]
-    scratch += [pltpu.VMEM((groups * capacity, p[1], by), f32) for p in PARTS]
     scratch += [pltpu.VMEM((2, n_f, 2 * bz // s, by), f32) for s in steps] * 2
     scratch += [pltpu.VMEM((n_f, bx // s, by), f32) for s in steps]
     scratch += [pltpu.VMEM((2, n_f, bx // s, by), f32) for s in steps]
@@ -433,16 +439,27 @@
     scratch += [pltpu.SemaphoreType.DMA((LEVELS, 2, 2))] * 2
     scratch += [pltpu.SemaphoreType.DMA((n_gz,))] * 2 + [pltpu.SemaphoreType.DMA((len(PARTS), groups))] * 2
     scratch += [pltpu.SemaphoreType.DMA((len(PARTS),))]
-    return pl.pallas_call(
+    coarse, *inbox = pl.pallas_call(
         functools.partial(kernel, (n_gx, n_gy, n_gz, n_f, bz, capacity)),
         out_shape=(jax.ShapeDtypeStruct((n_f, 2 * n_gz, 2, by // 8), f32),
-                   jax.ShapeDtypeStruct((groups * capacity, bx * by), f32)),
+                   *[jax.ShapeDtypeStruct((groups * capacity, p[1], by), f32) for p in PARTS]),
         in_specs=[pl.BlockSpec(memory_space=pltpu.SMEM)] + [pl.BlockSpec(memory_space=pltpu.HBM)] * 6,
-        out_specs=(pl.BlockSpec(memory_space=pltpu.VMEM), pl.BlockSpec(memory_space=pltpu.VMEM)),
+        out_specs=(pl.BlockSpec(memory_space=pltpu.VMEM), *[pl.BlockSpec(memory_space=pltpu.HBM)] * len(PARTS)),
         scratch_shapes=scratch,
         compiler_params=pltpu.CompilerParams(collective_id=0, has_side_effects=True,
                                              vmem_limit_bytes=60 * 1024 * 1024),
     )(source, fields, *tables)
+    rows = groups * capacity
+    block = 40 if rows % 40 == 0 else 64
+    bands = pl.BlockSpec(coarse.shape, lambda i: (0, 0, 0, 0))
+    return pl.pallas_call(
+        lay_out,
+        grid=(rows // block,),
+        out_shape=(jax.ShapeDtypeStruct(coarse.shape, f32), jax.ShapeDtypeStruct((rows, bx * by), f32)),
+        in_specs=[bands] + [pl.BlockSpec((block, p[1], by), lambda i: (i, 0, 0)) for p in PARTS],
+        out_specs=(bands, pl.BlockSpec((block, bx * by), lambda i: (i, 0))),
+        compiler_params=pltpu.CompilerParams(vmem_limit_bytes=60 * 1024 * 1024),
+    )(coarse, *inbox)
 
 
 def solution(mesh):

time: 51.8 us -> 50.9 us (0.983)
  local copies, waits for them, and re-layouts: 4.28 us -> 0.65 us
  Pallas kernels: 45.8 us -> 48.5 us
    unnamed x4 -> x2, local copies, waits for them, and re-layouts: 4.28 us -> 0.65 us
    pallas_call x0 -> x1, Pallas kernels: none -> 3.39 us  [body(): pl.pallas_call(lay_out, grid=(rows // block,), out_shape=(jax.ShapeDtypeS...]
    pallas_call x1, Pallas kernels: 45.8 us -> 45.1 us  [body(): pl.pallas_call(functools.partial(kernel, (n_gx, n_gy, n_gz, n_f, bz, capa...]
where the time goes in v7:
time: 50.9 us; the launch traced here: 50.6 us
  Pallas kernels  48.5 us (95%)
  other arithmetic  0.81 us (2%)
  between operations  0.66 us (1%)
  local copies, waits for them, and re-layouts  0.65 us (1%)
    pallas_call x1, Pallas kernels, body(): pl.pallas_call(functools.partial(kernel, (n_gx, n_gy, n_gz, n_f, bz, capa...  45.1 us
    pallas_call x1, Pallas kernels, body(): pl.pallas_call(lay_out, grid=(rows // block,), out_shape=(jax.ShapeDtypeS...  3.39 us

profile of v7, /device:TPU:0, one launch (start us, length us, event | category | flops | bytes accessed | tf_op | source)
XLA Modules:
  0.0 50.6 jit_solution(13025576694299583158)
XLA Ops:
  0.6 0.0 copy-start
  0.6 0.6 %copy-done = s32[1,1,80,1]{2,3,1,0:T(1,128)S(1)} copy-done((s32[1,1,80,1]{2,3,1,0:T(1,128)S(1)}, s32[1,1,80,1]{2,3,1,0:T(1,128)}, u32[]{:S(2)}) %copy-start) | copy-done | bytes 344
  1.3 0.2 convert_reduce_fusion
  1.5 0.1 select_reduce_fusion
  1.6 0.5 %broadcast_subtract_fusion.source_ref = s32[120]{0:T(128)} fusion(s32[120]{0:T(128)S(1)} %select_reduce_fusion), kind=kLoop, calls=%fused_computation.7 | loop fusion | flops 120 | bytes 960 | tf_op jit(solution)/shard_map/sub | solution.py:416
  2.1 45.1 %shard_map.86 = (f32[5,8,2,16]{3,2,1,0:T(2,128)}, f32[120,8,128]{2,1,0:T(8,128)}, f32[120,4,128]{2,1,0:T(4,128)}, f32[120,4,128]{2,1,0:T(4,128)}) custom-call(s32[120]{0:T(128)} %broadcast_subtract_fusion.source_ref, f32[5,16,16,128]{3,2,1,0:T(8,128)} %refs_0_.1, bf16[3,2,128,128]{3,2,1,0:T(8,128)(2,1)} %constant.18.clone.refs_1_, ...), custom_call_target="tpu_custom_call" | custom-call | tf_op jit(solution)/shard_map/pallas_call | solution.py:442
  47.2 3.4 %shard_map.87 = (f32[5,8,2,16]{3,2,1,0:T(2,128)}, f32[120,2048]{1,0:T(8,128)}) custom-call(f32[5,8,2,16]{3,2,1,0:T(2,128)} %get-tuple-element.6.coarse_ref, f32[120,8,128]{2,1,0:T(8,128)} %get-tuple-element.7.refs_0_, f32[120,4,128]{2,1,0:T(4,128)} %get-tuple-element.8.refs_1_, f32[120,4,128]{2,1,0:T(4,128)} %get-tuple-element.9.refs_2_), custom_call_target="tpu_custom_call" | custom-call | tf_op jit(solution)/shard_map/pallas_call | solution.py:455
  (1 shorter events, 0.0 us)
Async XLA Ops:
  0.6 0.7 %copy-start = (s32[1,1,80,1]{2,3,1,0:T(1,128)S(1)}, s32[1,1,80,1]{2,3,1,0:T(1,128)}, u32[]{:S(2)}) copy-start(s32[1,1,80,1]{2,3,1,0:T(1,128)} %param.8) | copy-start | bytes 964

commit v8 on v7

--- a/solution.py
+++ b/solution.py
@@ -400,7 +400,7 @@
         for part, (first, count, stride) in enumerate(PARTS):
             for x in range(count):
                 at = (first + stride * x) * 128
-                received_ref[rows, at:at + 128] = inbox[part][rows, x, :]
+                received_ref[rows, at:at + 128] = inbox[part][pl.ds(8 * k * count + x, 8, count), :]
         return carry
 
     lax.fori_loop(0, received_ref.shape[0] // 8, unpack, 0)
@@ -456,10 +456,10 @@
         lay_out,
         grid=(rows // block,),
         out_shape=(jax.ShapeDtypeStruct(coarse.shape, f32), jax.ShapeDtypeStruct((rows, bx * by), f32)),
-        in_specs=[bands] + [pl.BlockSpec((block, p[1], by), lambda i: (i, 0, 0)) for p in PARTS],
+        in_specs=[bands] + [pl.BlockSpec((block * p[1], by), lambda i: (i, 0)) for p in PARTS],
         out_specs=(bands, pl.BlockSpec((block, bx * by), lambda i: (i, 0))),
         compiler_params=pltpu.CompilerParams(vmem_limit_bytes=60 * 1024 * 1024),
-    )(coarse, *inbox)
+    )(coarse, *[part.reshape(-1, by) for part in inbox])
 
 
 def solution(mesh):

time: 50.9 us -> 50.6 us (level)
  no operation moved by 1% of the time
where the time goes in v8:
time: 50.6 us; the launch traced here: 50.4 us
  Pallas kernels  48.3 us (95%)
  other arithmetic  0.81 us (2%)
  between operations  0.66 us (1%)
  local copies, waits for them, and re-layouts  0.65 us (1%)
    pallas_call x1, Pallas kernels, body(): pl.pallas_call(functools.partial(kernel, (n_gx, n_gy, n_gz, n_f, bz, capa...  45.1 us
    pallas_call x1, Pallas kernels, body(): pl.pallas_call(lay_out, grid=(rows // block,), out_shape=(jax.ShapeDtypeS...  3.17 us

profile of v8, /device:TPU:0, one launch (start us, length us, event | category | flops | bytes accessed | tf_op | source)
XLA Modules:
  0.0 50.4 jit_solution(4002844071113528643)
XLA Ops:
  0.6 0.0 copy-start
  0.6 0.6 %copy-done = s32[1,1,80,1]{2,3,1,0:T(1,128)S(1)} copy-done((s32[1,1,80,1]{2,3,1,0:T(1,128)S(1)}, s32[1,1,80,1]{2,3,1,0:T(1,128)}, u32[]{:S(2)}) %copy-start) | copy-done | bytes 344
  1.3 0.2 convert_reduce_fusion
  1.5 0.1 select_reduce_fusion
  1.6 0.5 %broadcast_subtract_fusion.source_ref = s32[120]{0:T(128)} fusion(s32[120]{0:T(128)S(1)} %select_reduce_fusion), kind=kLoop, calls=%fused_computation.7 | loop fusion | flops 120 | bytes 960 | tf_op jit(solution)/shard_map/sub | solution.py:416
  2.1 45.1 %shard_map.86 = (f32[5,8,2,16]{3,2,1,0:T(2,128)}, f32[120,8,128]{2,1,0:T(8,128)}, f32[120,4,128]{2,1,0:T(4,128)}, f32[120,4,128]{2,1,0:T(4,128)}) custom-call(s32[120]{0:T(128)} %broadcast_subtract_fusion.source_ref, f32[5,16,16,128]{3,2,1,0:T(8,128)} %refs_0_.1, bf16[3,2,128,128]{3,2,1,0:T(8,128)(2,1)} %constant.18.clone.refs_1_, ...), custom_call_target="tpu_custom_call" | custom-call | tf_op jit(solution)/shard_map/pallas_call | solution.py:442
  47.2 3.2 %shard_map.87 = (f32[5,8,2,16]{3,2,1,0:T(2,128)}, f32[120,2048]{1,0:T(8,128)}) custom-call(f32[5,8,2,16]{3,2,1,0:T(2,128)} %get-tuple-element.6.coarse_ref, f32[960,128]{1,0:T(8,128)} %bitcast.5, f32[480,128]{1,0:T(8,128)} %bitcast.6, f32[480,128]{1,0:T(8,128)} %bitcast.7), custom_call_target="tpu_custom_call" | custom-call | tf_op jit(solution)/shard_map/pallas_call | solution.py:455
  (1 shorter events, 0.0 us)
Async XLA Ops:
  0.6 0.7 %copy-start = (s32[1,1,80,1]{2,3,1,0:T(1,128)S(1)}, s32[1,1,80,1]{2,3,1,0:T(1,128)}, u32[]{:S(2)}) copy-start(s32[1,1,80,1]{2,3,1,0:T(1,128)} %param.8) | copy-start | bytes 964

commit v9 on v8

--- a/solution.py
+++ b/solution.py
@@ -158,10 +158,13 @@
     def exchange(level, kind, f, way):
         axis = ("gx", "gy", "gz")[kind]
         out, into = ((xs, xr), (ys, yr), (zs, zr))[kind]
-        src = out[level].at[f] if kind == 1 else out[level].at[way, f]
+        src = out[level] if kind == 1 else out[level].at[way]
+        dst = into[level].at[way]
+        if level < 2:
+            src, dst = src.at[f], dst.at[f]
         row = level * 3 + kind
         return pltpu.make_async_remote_copy(
-            src_ref=src, dst_ref=into[level].at[way, f],
+            src_ref=src, dst_ref=dst,
             send_sem=send.at[row, way, f], recv_sem=recv.at[row, way, f],
             device_id={axis: beside(axis, way)}, device_id_type=MESH)
 
@@ -180,9 +183,9 @@
         for k in range(0, len(tiles), t):
             edge = product(sums, halves(jnp.concatenate(tiles[k:k + t], axis=0)))
             for way in range(2):
-                xs[level][way, f, 2 * k:2 * (k + t), :] = edge[2 * t * way:2 * t * (way + 1)]
-        for way in range(2):
-            exchange(level, 0, f, way).start()
+                    xs[level][way, f, 2 * k:2 * (k + t), :] = edge[2 * t * way:2 * t * (way + 1)]
+        if level < 2:
+            per_field(level, f, start, [0])
 
     def spot(i, step):
         return i // step * (8 * step) + i % step
@@ -204,6 +207,25 @@
     def put(f, step, tiles):
         for i, tile in enumerate(tiles):
             work[f * bz + i * step] = tile
+
+    def per_field(level, f, act, kinds):
+        if level < 2 or (isinstance(f, int) and f == 0):
+            for kind in kinds:
+                for way in range(2):
+                    act(exchange(level, kind, f, way))
+
+    def start(copy):
+        copy.start()
+
+    def arrive(copy):
+        copy.wait_recv()
+
+    def stage(level, body):
+        if level < 2:
+            loop(body)
+        else:
+            for f in range(n_f):
+                body(f)
 
     def loop(body):
         def run(f, carry):
@@ -262,8 +284,7 @@
 
         def x_stage(f, level=level, step=step, t=t, live=live):
             tiles = planes(f, step, fields_ref if level == 0 else work)
-            for way in range(2):
-                exchange(level, 0, f, way).wait_recv()
+            per_field(level, f, arrive, [0])
             mx = tuple(mx_ref[level, half, :16 * t, :16 * t] for half in range(2))
             hx = tuple(hx_ref[level, half, :16 * t, :4 * t] for half in range(2))
             mq = tuple(mq_ref[level, half] for half in range(2))
@@ -283,16 +304,19 @@
                 else:
                     mixed = jnp.where(lane % step == 0, sums[way][0], pltpu.roll(sums[way][1], 1, 1))
                     zs[level][way, f] = squeeze(way, mixed, step)
-                exchange(level, 2, f, way).start()
+            if level < 2:
+                per_field(level, f, start, [2])
             pack = packed(step, list(enumerate(sum_lanes)), jnp.zeros((16, 128), jnp.float32))
             ys[level][f] = squeeze(2, pack, step)
-            for way in range(2):
-                exchange(level, 1, f, way).start()
+            if level < 2:
+                per_field(level, f, start, [1])
             sums = edge_sums(lambda k: sum_lanes[k], len(wide))
             for way in range(2):
                 cs[level][way] = packed(step, [(2 * f + j, sums[way][j]) for j in range(2)], cs[level][way])
 
-        loop(x_stage)
+        stage(level, x_stage)
+        if level == 2:
+            per_field(level, 0, start, [2, 1])
         for yway in range(2):
             for zway in range(2):
                 corner(level, yway, zway).start()
@@ -307,9 +331,7 @@
 
         def z_stage(f, level=level, step=step, live=live):
             old = planes(f, step, work)
-            for way in range(2):
-                exchange(level, 1, f, way).wait_recv()
-                exchange(level, 2, f, way).wait_recv()
+            per_field(level, f, arrive, [1, 2])
             hy = tuple(hy_ref[level, half] for half in range(2))
             edges = edge_lanes(step, spread(3, yr[level][0, f], step), spread(4, yr[level][1, f], step), range(len(old)))
             for way in range(2):
@@ -334,7 +356,9 @@
             if level + 1 < LEVELS:
                 send_x(level + 1, f, new[::2])
 
-        loop(z_stage)
+        stage(level, z_stage)
+        if level == 1:
+            per_field(2, 0, start, [0])
 
     def gather(k):
         return pltpu.make_async_remote_copy(
@@ -379,12 +403,13 @@
         gather(k).wait_send()
 
     def sent(f):
-        for level in range(LEVELS):
+        for level in range(2):
             for kind in range(3):
                 for way in range(2):
                     exchange(level, kind, f, way).wait_send()
 
     loop(sent)
+    per_field(2, 0, lambda copy: copy.wait_send(), range(3))
     for level in range(LEVELS):
         for yway in range(2):
             for zway in range(2):

time: 50.6 us -> 51.2 us (1.012)
    pallas_call x1, Pallas kernels: 45.1 us -> 45.7 us  [body(): pl.pallas_call(functools.partial(kernel, (n_gx, n_gy, n_gz, n_f, bz, capa...]
where the time goes in v9:
time: 51.2 us; the launch traced here: 51 us
  Pallas kernels  48.8 us (95%)
  other arithmetic  0.81 us (2%)
  between operations  0.66 us (1%)
  local copies, waits for them, and re-layouts  0.65 us (1%)
    pallas_call x1, Pallas kernels, body(): pl.pallas_call(functools.partial(kernel, (n_gx, n_gy, n_gz, n_f, bz, capa...  45.7 us
    pallas_call x1, Pallas kernels, body(): pl.pallas_call(lay_out, grid=(rows // block,), out_shape=(jax.ShapeDtypeS...  3.17 us

profile of v9, /device:TPU:0, one launch (start us, length us, event | category | flops | bytes accessed | tf_op | source)
XLA Modules:
  0.0 51.0 jit_solution(10794167649723398687)
XLA Ops:
  0.6 0.0 copy-start
  0.6 0.6 %copy-done = s32[1,1,80,1]{2,3,1,0:T(1,128)S(1)} copy-done((s32[1,1,80,1]{2,3,1,0:T(1,128)S(1)}, s32[1,1,80,1]{2,3,1,0:T(1,128)}, u32[]{:S(2)}) %copy-start) | copy-done | bytes 344
  1.3 0.2 convert_reduce_fusion
  1.5 0.1 select_reduce_fusion
  1.6 0.5 %broadcast_subtract_fusion.source_ref = s32[120]{0:T(128)} fusion(s32[120]{0:T(128)S(1)} %select_reduce_fusion), kind=kLoop, calls=%fused_computation.7 | loop fusion | flops 120 | bytes 960 | tf_op jit(solution)/shard_map/sub | solution.py:441
  2.1 45.7 %shard_map.86 = (f32[5,8,2,16]{3,2,1,0:T(2,128)}, f32[120,8,128]{2,1,0:T(8,128)}, f32[120,4,128]{2,1,0:T(4,128)}, f32[120,4,128]{2,1,0:T(4,128)}) custom-call(s32[120]{0:T(128)} %broadcast_subtract_fusion.source_ref, f32[5,16,16,128]{3,2,1,0:T(8,128)} %refs_0_.1, bf16[3,2,128,128]{3,2,1,0:T(8,128)(2,1)} %constant.18.clone.refs_1_, ...), custom_call_target="tpu_custom_call" | custom-call | tf_op jit(solution)/shard_map/pallas_call | solution.py:467
  47.8 3.2 %shard_map.87 = (f32[5,8,2,16]{3,2,1,0:T(2,128)}, f32[120,2048]{1,0:T(8,128)}) custom-call(f32[5,8,2,16]{3,2,1,0:T(2,128)} %get-tuple-element.6.coarse_ref, f32[960,128]{1,0:T(8,128)} %bitcast.5, f32[480,128]{1,0:T(8,128)} %bitcast.6, f32[480,128]{1,0:T(8,128)} %bitcast.7), custom_call_target="tpu_custom_call" | custom-call | tf_op jit(solution)/shard_map/pallas_call | solution.py:480
  (1 shorter events, 0.0 us)
Async XLA Ops:
  0.6 0.7 %copy-start = (s32[1,1,80,1]{2,3,1,0:T(1,128)S(1)}, s32[1,1,80,1]{2,3,1,0:T(1,128)}, u32[]{:S(2)}) copy-start(s32[1,1,80,1]{2,3,1,0:T(1,128)} %param.8) | copy-start | bytes 964
